TPU v7x, 512 devices: a whole 4x8x8 slice. The times are simulated.
512 devices in a mesh: rep: 64 (over z_lo, y, core), tp: 8 (over x, z_hi).
Axes of the slice: x: 4, y: 8, z: 8 (z_hi: 2, z_lo: 4; z = z_hi * 4 + z_lo), core: 2. Of those that a mesh axis runs over, the one named last changes fastest.
Arguments:
- activations: bfloat16 [64, 1024, 256], P('rep', 'tp'), may hold values from -6 to 6
- out_grads: bfloat16 [64, 1024, 4096], P('rep', None, 'tp'), may hold values from -6 to 6
- weight: bfloat16 [64, 256, 4096], P('rep', None, 'tp'), may hold values from -6 to 6
- public: bfloat16 [64, 256, 4096], P('rep', None, 'tp'), may hold values from -6 to 6
- counts: int32 [64], P('rep'), may hold values from 256 to 1024, as said below
- kept: int32 [64, 8, 40], P('rep', 'tp'), may hold values from 0 to 63, as said below
- distances: int32 [2], replicated, may hold values from 1 to 32, as said below
Outputs:
- new_weight: bfloat16 [64, 256, 4096], P('rep', None, 'tp')
Inputs may be any that keep to these rules, and one draw needn't show every extreme that they name: `counts`: at least 256; some replica has exactly 1024. `kept`: the 40 indices of each replica and shard are distinct. `distances`: powers of two, the same for every replica; the rounds' distances differ, and one of the rounds has distance half the number of replicas.
All inputs are finite; a program needn't handle non-finite values.
Results may differ from a plain program's by a relative error of at most 0.006.
Values may be sent and summed in bfloat16 or wider, within the bound.
No kernel may reach another device: no remote copies, remote signals or barrier semaphores. Data moves between devices by JAX's collectives and lax.ppermute only.
A program may use at most 128 MiB of HBM per device.

v0:
```python
import jax
import jax.numpy as jnp
from jax import lax
from jax.sharding import PartitionSpec as P

ROUNDS = 2


learn_rate = 0.02
mix_weight = 0.5
highest = lax.Precision.HIGHEST


def for_sending(x):

    def short(part):
        return part.astype(jnp.bfloat16) if part.dtype == jnp.float32 else part

    return jax.tree.map(short, x)


def swapped(block, axis, apart):
    count = lax.axis_size(axis)
    route = []
    for low in range(count):
        high = low | 1 << apart
        if high != low and high < count:
            route += [(low, high), (high, low)]
    return lax.ppermute(block, axis, route)


def cosine_table():
    freqs = jnp.arange(64, dtype=jnp.float32)[:, None]
    places = jnp.arange(64, dtype=jnp.float32)[None, :]
    scales = jnp.where(
        freqs == 0.0, jnp.sqrt(jnp.float32(1.0 / 64.0)), jnp.sqrt(jnp.float32(2.0 / 64.0))
    )
    return scales * jnp.cos(jnp.pi * (2.0 * places + 1.0) * freqs / 128.0)


def transform_forward(residual, table, paired):
    rows_total, cols_total = residual.shape
    stacked = residual.reshape(rows_total // 64, 64, cols_total)
    left_side = jnp.einsum("un,anc->auc", table, stacked, precision=highest)
    right_side = jnp.dot(left_side.reshape(-1, 128), paired.T, precision=highest)
    return right_side.reshape(rows_total // 64, 64, cols_total)


def transform_inverse(coeffs, table, paired):
    tile_rows, sixty_four, cols_total = coeffs.shape
    left_side = jnp.einsum("un,auc->anc", table, coeffs, precision=highest)
    right_side = jnp.dot(left_side.reshape(-1, 128), paired, precision=highest)
    return right_side.reshape(tile_rows * 64, cols_total)


def swap_copies(operand, bit_index, levels):

    def make_swap(level_bit):
        return lambda tiles_in: jax.tree.map(
            lambda part, own: part.astype(own.dtype),
            swapped(for_sending(tiles_in), "rep", level_bit),
            tiles_in,
        )

    return lax.switch(bit_index, [make_swap(level_bit) for level_bit in range(levels)], operand)


def level_of(distance, levels):
    return sum(((distance > 1 << level_bit).astype(jnp.int32) for level_bit in range(levels)))


def shards(activations, out_grads, weight, public, counts, kept, distances):
    levels = lax.axis_size("rep").bit_length() - 1
    bit_indices = [level_of(distances[round_index], levels) for round_index in range(ROUNDS)]
    cols_local = weight.shape[2]
    table = cosine_table()
    paired = jnp.kron(jnp.eye(2, dtype=jnp.float32), table)
    kept_local = kept[0, 0]
    row_blocks = jnp.arange(64, dtype=jnp.int32)[:, None] // 8
    col_blocks = jnp.arange(cols_local, dtype=jnp.int32)[None, :] % 64 // 8
    index_grid = row_blocks * 8 + col_blocks
    keep_mask = jnp.any(kept_local[:, None, None] == index_grid[None], axis=0).astype(jnp.float32)
    token_count = counts[0]
    total_tokens = out_grads.shape[1]
    live_rows = (jnp.arange(total_tokens, dtype=jnp.int32) < token_count).astype(jnp.bfloat16)
    grads_live = out_grads[0] * live_rows[:, None]
    gradient = lax.dot_general(
        lax.all_gather(activations[0], "tp", axis=0, tiled=True),
        grads_live,
        (((0,), (0,)), ((), ())),
        preferred_element_type=jnp.float32,
    )
    weights_now = weight[0].astype(jnp.float32) - learn_rate * gradient
    public_now = public[0].astype(jnp.float32)
    for round_index in range(ROUNDS):
        bit_index = bit_indices[round_index]
        coeffs = transform_forward(weights_now - public_now, table, paired) * keep_mask[None]
        update_own = transform_inverse(coeffs, table, paired)
        public_now = public_now + update_own
        peer_copy = swap_copies(public_now, bit_index, levels)
        weights_now = weights_now + mix_weight * 0.5 * (peer_copy - public_now)
    return weights_now.astype(jnp.bfloat16)[None]


def solution(mesh):
    return jax.shard_map(
        shards,
        mesh=mesh,
        in_specs=(
            P("rep", "tp", None),
            P("rep", None, "tp"),
            P("rep", None, "tp"),
            P("rep", None, "tp"),
            P("rep"),
            P("rep", "tp", None),
            P(),
        ),
        out_specs=P("rep", None, "tp"),
        check_vma=False,
    )
```

profile of v0, /device:TPU:40, one launch (start us, length us, event | category | flops | bytes accessed | tf_op | source)
XLA Modules:
  0.0 97.3 jit_solution(9251980831747317814)
XLA Ops:
  0.8 1.4 %fusion.38 = (s32[1]{0:T(128)}, s32[1]{0:T(128)}) fusion(s32[2]{0:T(128)} %param.25), kind=kLoop, calls=%fused_computation.67 | loop fusion | bytes 16 | tf_op jit(solution)/shard_map/slice | solution.py:74
  10.3 0.2 cosine_multiply_fusion
  10.5 0.1 copy.12
  10.5 0.1 broadcast_multiply_fusion
  10.7 0.1 mul.278
  10.8 0.1 broadcast_add_fusion
  10.9 1.4 %compare_reduce_fusion = pred[64,512]{1,0:T(8,128)(4,1)S(1)} fusion(s32[64,512]{1,0:T(8,128)S(1)} %broadcast_add_fusion, s32[40]{0:T(128)} %bitcast.61), kind=kLoop, calls=%fused_computation | loop fusion | flops 2588672 | bytes 164000 | tf_op jit(solution)/shard_map/reduce_or | solution.py:82
  12.3 53.4 %all-gather = bf16[1,1024,256]{2,1,0:T(8,128)(2,1)S(1)} all-gather(bf16[1,128,256]{2,1,0:T(8,128)(2,1)} %param.19), channel_id=2, replica_groups=mesh['rep'=64,'tp'=8] {'tp'}, dimensions={1}, use_global_device_ids=true | all-gather | bytes 589824 | tf_op jit(solution)/shard_map/all_gather | solution.py:88
  65.7 0.6 convert_subtract_fusion
  66.3 0.8 convolution_bitcast_fusion.3
  67.2 0.6 fusion.39
  67.8 0.1 reshape.289
  67.9 0.8 convolution_bitcast_fusion.2
  68.8 0.6 fusion.40
  69.3 0.1 reshape.291
  69.4 0.3 copy-done.2
  69.7 0.1 convert_add_fusion
  69.8 14.0 %conditional.8 = (f32[256,512]{1,0:T(8,128)S(1)}) conditional(s32[]{:T(128)} %bitcast.5, f32[256,512]{1,0:T(8,128)S(1)} %convert_add_fusion, f32[256,512]{1,0:T(8,128)S(1)} %convert_add_fusion, f32[256,512]{1,0:T(8,128)S(1)} %convert_add_fusion, f32[256,512]{1,0:T(8,128)S(1)} %convert_add_fusion, ...), branch_computations={%region_1.2_spmd, %region_2.3_spmd, %region_3.4_spmd, %region_4.5_... | conditional | flops 262144 | bytes 2621488
  69.9 7.7 %collective-permute-start.5 = (bf16[256,512]{1,0:T(8,128)(2,1)S(1)}, bf16[256,512]{1,0:T(8,128)(2,1)S(1)}, u32[]{:S(2)}, u32[]{:S(2)}) collective-permute-start(bf16[256,512]{1,0:T(8,128)(2,1)S(1)} %convert_element_type.159), channel_id=1, source_target_pairs={{0,256},{256,0},{8,264},{264,8},{16,272},{272,16},{24,280},{280,24... | collective-permute-start | bytes 786440 | tf_op jit(solution)/shard_map/cond/branch_5_fun/ppermute | solution.py:29
  77.6 6.1 %collective-permute-done.5 = bf16[256,512]{1,0:T(8,128)(2,1)S(1)} collective-permute-done((bf16[256,512]{1,0:T(8,128)(2,1)S(1)}, bf16[256,512]{1,0:T(8,128)(2,1)S(1)}, u32[]{:S(2)}, u32[]{:S(2)}) %collective-permute-start.5) | collective-permute-done | bytes 262176 | tf_op jit(solution)/shard_map/cond/branch_5_fun/ppermute | solution.py:29
  83.8 0.2 fusion.9
  83.9 0.8 convolution_bitcast_fusion.1
  84.8 0.6 fusion.41
  85.4 0.1 reshape.294
  85.5 0.8 convolution_bitcast_fusion
  86.4 0.6 fusion.42
  86.9 0.1 reshape.296
  87.0 0.1 add.171
  87.1 9.2 %conditional.9 = (f32[256,512]{1,0:T(8,128)S(1)}) conditional(s32[]{:T(128)} %bitcast.14, f32[256,512]{1,0:T(8,128)S(1)} %add.171, f32[256,512]{1,0:T(8,128)S(1)} %add.171, f32[256,512]{1,0:T(8,128)S(1)} %add.171, f32[256,512]{1,0:T(8,128)S(1)} %add.171, f32[256,512]{1,0:T(8,128)S(1)} %add.171, ...), branch_computations={%region_7.8_spmd, %region_8.9_spmd, %region_9.10_spmd, %region_10.... | conditional | flops 262144 | bytes 2621488
  87.2 1.9 %collective-permute-start.10 = (bf16[256,512]{1,0:T(8,128)(2,1)S(1)}, bf16[256,512]{1,0:T(8,128)(2,1)S(1)}, u32[]{:S(2)}, u32[]{:S(2)}) collective-permute-start(bf16[256,512]{1,0:T(8,128)(2,1)S(1)} %convert_element_type.169), channel_id=1, source_target_pairs={{0,128},{128,0},{8,136},{136,8},{16,144},{144,16},{24,152},{152,24... | collective-permute-start | bytes 786440 | tf_op jit(solution)/shard_map/cond/branch_4_fun/ppermute | solution.py:29
  89.1 7.1 %collective-permute-done.10 = bf16[256,512]{1,0:T(8,128)(2,1)S(1)} collective-permute-done((bf16[256,512]{1,0:T(8,128)(2,1)S(1)}, bf16[256,512]{1,0:T(8,128)(2,1)S(1)}, u32[]{:S(2)}, u32[]{:S(2)}) %collective-permute-start.10) | collective-permute-done | bytes 262176 | tf_op jit(solution)/shard_map/cond/branch_4_fun/ppermute | solution.py:29
  96.3 1.0 %fusion.6 = bf16[1,256,512]{2,1,0:T(8,128)(2,1)} fusion(f32[256,512]{1,0:T(8,128)S(1)} %get-tuple-element.50, f32[256,512]{1,0:T(8,128)S(1)} %add.171, f32[256,512]{1,0:T(8,128)S(1)} %get-tuple-element.46, f32[256,512]{1,0:T(8,128)S(1)} %get-tuple-element.49, f32[256,512]{1,0:T(8,128)S(1)} %convert_add_fusion), kind=kLoop, calls=%fused_computation.17 | loop fusion | flops 917504 | bytes 2883584 | tf_op jit(solution)/shard_map/broadcast_in_dim | solution.py:102
  (21 shorter events, 0.4 us)
Async XLA Ops:
  0.0 65.7 %copy-start.1 = (bf16[1,256,512]{2,1,0:T(8,128)(2,1)S(1)}, bf16[1,256,512]{2,1,0:T(8,128)(2,1)}, u32[]{:S(2)}) copy-start(bf16[1,256,512]{2,1,0:T(8,128)(2,1)} %param.22) | copy-start | bytes 786436
  0.0 65.7 %copy-start = (bf16[1,1024,512]{2,1,0:T(8,128)(2,1)S(1)}, bf16[1,1024,512]{2,1,0:T(8,128)(2,1)}, u32[]{:S(2)}) copy-start(bf16[1,1024,512]{2,1,0:T(8,128)(2,1)} %param.20) | copy-start | bytes 3145732
  10.8 54.9 %copy-start.3 = (bf16[1,256,512]{2,1,0:T(8,128)(2,1)S(1)}, bf16[1,256,512]{2,1,0:T(8,128)(2,1)}, u32[]{:S(2)}) copy-start(bf16[1,256,512]{2,1,0:T(8,128)(2,1)} %param.21) | copy-start | bytes 786436
  68.8 1.0 copy-start.2
  69.9 13.8 %collective-permute-start.5 = (bf16[256,512]{1,0:T(8,128)(2,1)S(1)}, bf16[256,512]{1,0:T(8,128)(2,1)S(1)}, u32[]{:S(2)}, u32[]{:S(2)}) collective-permute-start(bf16[256,512]{1,0:T(8,128)(2,1)S(1)} %convert_element_type.159), channel_id=1, source_target_pairs={{0,256},{256,0},{8,264},{264,8},{16,272},{272,16},{24,280},{280,24... | collective-permute-start | bytes 786440 | tf_op jit(solution)/shard_map/cond/branch_5_fun/ppermute | solution.py:29
  87.2 9.0 %collective-permute-start.10 = (bf16[256,512]{1,0:T(8,128)(2,1)S(1)}, bf16[256,512]{1,0:T(8,128)(2,1)S(1)}, u32[]{:S(2)}, u32[]{:S(2)}) collective-permute-start(bf16[256,512]{1,0:T(8,128)(2,1)S(1)} %convert_element_type.169), channel_id=1, source_target_pairs={{0,128},{128,0},{8,136},{136,8},{16,144},{144,16},{24,152},{152,24... | collective-permute-start | bytes 786440 | tf_op jit(solution)/shard_map/cond/branch_4_fun/ppermute | solution.py:29
where the time goes:
time: 97.6 us; the launch traced here: 97.3 us
  blocking collectives  53.4 us (55%)
  waiting for transfers between devices  13.2 us (14%)
  starting transfers between devices  9.61 us (10%)
  between operations  9.06 us (9%)
  matrix products  6.21 us (6%)
  other arithmetic  3.31 us (3%)
  local copies, waits for them, and re-layouts  2.36 us (2%)
    all_gather x1, blocking collectives, shards(): lax.all_gather(activations[0], 'tp', axis=0, tiled=True)  53.4 us
    ppermute x2, waiting for transfers between devices, swapped(): return lax.ppermute(block, axis, route)  13.2 us
    ppermute x2, starting transfers between devices, swapped(): return lax.ppermute(block, axis, route)  9.61 us
  transfers between devices with their start and end apart: 2, of which 2 were waited for; matrix products, arithmetic and copies ran while one was open for 0% of the time, Pallas kernels for 0%

commit v1 on v0

--- a/solution.py
+++ b/solution.py
@@ -27,6 +27,12 @@
         if high != low and high < count:
             route += [(low, high), (high, low)]
     return lax.ppermute(block, axis, route)
+
+
+def gathered(block):
+    count = lax.axis_size("tp")
+    copies = jnp.broadcast_to(block[None], (count,) + block.shape)
+    return lax.all_to_all(copies, "tp", 0, 0).reshape(-1, block.shape[1])
 
 
 def cosine_table():
@@ -65,13 +71,9 @@
     return lax.switch(bit_index, [make_swap(level_bit) for level_bit in range(levels)], operand)
 
 
-def level_of(distance, levels):
-    return sum(((distance > 1 << level_bit).astype(jnp.int32) for level_bit in range(levels)))
-
-
 def shards(activations, out_grads, weight, public, counts, kept, distances):
     levels = lax.axis_size("rep").bit_length() - 1
-    bit_indices = [level_of(distances[round_index], levels) for round_index in range(ROUNDS)]
+    bit_indices = lax.population_count(distances - 1)
     cols_local = weight.shape[2]
     table = cosine_table()
     paired = jnp.kron(jnp.eye(2, dtype=jnp.float32), table)
@@ -85,7 +87,7 @@
     live_rows = (jnp.arange(total_tokens, dtype=jnp.int32) < token_count).astype(jnp.bfloat16)
     grads_live = out_grads[0] * live_rows[:, None]
     gradient = lax.dot_general(
-        lax.all_gather(activations[0], "tp", axis=0, tiled=True),
+        gathered(activations[0]),
         grads_live,
         (((0,), (0,)), ((), ())),
         preferred_element_type=jnp.float32,

time: 97.6 us -> 75.9 us (0.78)
  the two profiles are of different devices: /device:TPU:40 before, /device:TPU:1 now
where the time goes in v1:
time: 75.9 us; the launch traced here: 75.4 us
  waiting for transfers between devices  32.6 us (43%)
  starting transfers between devices  28.6 us (38%)
  matrix products  6.22 us (8%)
  local copies, waits for them, and re-layouts  3 us (4%)
  other arithmetic  2.67 us (4%)
  between operations  2.17 us (3%)
    ppermute x2, waiting for transfers between devices, swapped(): return lax.ppermute(block, axis, route)  23.3 us
    ppermute x2, starting transfers between devices, swapped(): return lax.ppermute(block, axis, route)  15.2 us
    all_to_all x1, starting transfers between devices, gathered(): return lax.all_to_all(copies, 'tp', 0, 0).reshape(-1, block.shape[1])  13.4 us
    all_to_all x1, waiting for transfers between devices, gathered(): return lax.all_to_all(copies, 'tp', 0, 0).reshape(-1, block.shape[1])  9.3 us
    broadcast_in_dim x1, local copies, waits for them, and re-layouts, gathered(): copies = jnp.broadcast_to(block[None], (count,) + block.shape)  1.7 us
    dot_general x2, matrix products, transform_forward(): left_side = jnp.einsum('un,anc->auc', table, stacked, precision=highest)  1.65 us
    dot_general x2, matrix products, transform_inverse(): left_side = jnp.einsum('un,auc->anc', table, coeffs, precision=highest)  1.63 us
  transfers between devices with their start and end apart: 3, of which 3 were waited for; matrix products, arithmetic and copies ran while one was open for 3% of the time, Pallas kernels for 0%

profile of v1, /device:TPU:1, one launch (start us, length us, event | category | flops | bytes accessed | tf_op | source)
XLA Modules:
  0.0 75.4 jit_solution(14502456674388347857)
XLA Ops:
  0.0 1.7 %broadcast_in_dim.19 = bf16[8,128,256]{2,1,0:T(8,128)(2,1)} broadcast(bf16[128,256]{1,0:T(8,128)(2,1)} %bitcast.60), dimensions={1,2} | broadcast | bytes 589824 | tf_op jit(solution)/shard_map/broadcast_in_dim | solution.py:34
  1.7 13.4 %all-to-all-start = ((bf16[8,128,256]{2,1,0:T(8,128)(2,1)}), bf16[8,128,256]{2,1,0:T(8,128)(2,1)S(1)}, u32[]{:S(2)}, u32[]{:S(2)}) async-start(bf16[8,128,256]{2,1,0:T(8,128)(2,1)} %broadcast_in_dim.19), calls=%async_computation | async-start | bytes 1048576 | tf_op jit(solution)/shard_map/all_to_all | solution.py:35
  15.8 0.6 fusion.39
  17.7 0.2 cosine_multiply_fusion
  17.9 0.1 copy.12
  18.0 0.1 broadcast_multiply_fusion
  18.1 0.1 mul.282
  18.2 0.1 broadcast_add_fusion
  18.3 0.7 compare_reduce_fusion
  19.1 9.3 %all-to-all-done = bf16[8,128,256]{2,1,0:T(8,128)(2,1)S(1)} async-done(((bf16[8,128,256]{2,1,0:T(8,128)(2,1)}), bf16[8,128,256]{2,1,0:T(8,128)(2,1)S(1)}, u32[]{:S(2)}, u32[]{:S(2)}) %all-to-all-start) | async-done | bytes 524320 | tf_op jit(solution)/shard_map/all_to_all | solution.py:35
  28.4 0.6 convert_subtract_fusion
  29.1 0.8 %convolution_bitcast_fusion.3 = f32[4,64,512]{2,1,0:T(8,128)S(1)} fusion(f32[4,64,512]{2,1,0:T(8,128)S(1)} %bitcast.57, f32[64]{0:T(128)S(1)} %get-tuple-element.48, f32[64]{0:T(128)S(1)} %get-tuple-element.47), kind=kOutput, calls=%fused_computation.7 | convolution fusion | flops 100675584 | bytes 1049088 | tf_op jit(solution)/shard_map/un,anc->auc/dot_general | solution.py:50
  30.0 0.6 fusion.40
  30.5 0.1 reshape.261
  30.6 0.8 %convolution_bitcast_fusion.2 = f32[4,64,512]{2,1,0:T(8,128)S(1)} fusion(f32[4,64,512]{2,1,0:T(8,128)S(1)} %reshape.261, f32[64,512]{1,0:T(8,128)S(1)} %convert_element_type.148, f32[64]{0:T(128)S(1)} %get-tuple-element.48, f32[64]{0:T(128)S(1)} %get-tuple-element.47), kind=kOutput, calls=%fused_computation.6 | convolution fusion | flops 100806656 | bytes 1180160 | tf_op jit(solution)/shard_map/un,auc->anc/dot_general | solution.py:57
  31.5 0.6 fusion.41
  32.1 0.1 reshape.263
  32.2 15.7 %conditional.8 = (f32[256,512]{1,0:T(8,128)S(1)}) conditional(s32[]{:T(128)} %bitcast.6, f32[256,512]{1,0:T(8,128)S(1)} %convert_add_fusion, f32[256,512]{1,0:T(8,128)S(1)} %convert_add_fusion, f32[256,512]{1,0:T(8,128)S(1)} %convert_add_fusion, f32[256,512]{1,0:T(8,128)S(1)} %convert_add_fusion, ...), branch_computations={%region_1.2_spmd, %region_2.3_spmd, %region_3.4_spmd, %region_4.5_... | conditional | flops 262144 | bytes 2621488
  32.3 4.2 %collective-permute-start.2 = (bf16[256,512]{1,0:T(8,128)(2,1)S(1)}, bf16[256,512]{1,0:T(8,128)(2,1)S(1)}, u32[]{:S(2)}, u32[]{:S(2)}) collective-permute-start(bf16[256,512]{1,0:T(8,128)(2,1)S(1)} %convert_element_type.111), channel_id=1, source_target_pairs={{0,32},{32,0},{8,40},{40,8},{16,48},{48,16},{24,56},{56,24},{64,96... | collective-permute-start | bytes 786440 | tf_op jit(solution)/shard_map/cond/branch_2_fun/ppermute | solution.py:29
  36.5 11.3 %collective-permute-done.2 = bf16[256,512]{1,0:T(8,128)(2,1)S(1)} collective-permute-done((bf16[256,512]{1,0:T(8,128)(2,1)S(1)}, bf16[256,512]{1,0:T(8,128)(2,1)S(1)}, u32[]{:S(2)}, u32[]{:S(2)}) %collective-permute-start.2) | collective-permute-done | bytes 262176 | tf_op jit(solution)/shard_map/cond/branch_2_fun/ppermute | solution.py:29
  47.9 0.2 fusion.10
  48.1 0.8 %convolution_bitcast_fusion.1 = f32[4,64,512]{2,1,0:T(8,128)S(1)} fusion(f32[4,64,512]{2,1,0:T(8,128)S(1)} %bitcast.58, f32[64]{0:T(128)S(1)} %get-tuple-element.48, f32[64]{0:T(128)S(1)} %get-tuple-element.47), kind=kOutput, calls=%fused_computation.5 | convolution fusion | flops 100675584 | bytes 1049088 | tf_op jit(solution)/shard_map/un,anc->auc/dot_general | solution.py:50
  49.0 0.6 fusion.42
  49.6 0.1 reshape.266
  49.7 0.8 %convolution_bitcast_fusion = f32[4,64,512]{2,1,0:T(8,128)S(1)} fusion(f32[4,64,512]{2,1,0:T(8,128)S(1)} %reshape.266, f32[64,512]{1,0:T(8,128)S(1)} %convert_element_type.148, f32[64]{0:T(128)S(1)} %get-tuple-element.48, f32[64]{0:T(128)S(1)} %get-tuple-element.47), kind=kOutput, calls=%fused_computation.4 | convolution fusion | flops 100806656 | bytes 1180160 | tf_op jit(solution)/shard_map/un,auc->anc/dot_general | solution.py:57
  50.5 0.6 fusion.43
  51.1 0.1 reshape.268
  51.2 0.1 add.122
  51.3 23.1 %conditional.9 = (f32[256,512]{1,0:T(8,128)S(1)}) conditional(s32[]{:T(128)} %bitcast.15, f32[256,512]{1,0:T(8,128)S(1)} %add.122, f32[256,512]{1,0:T(8,128)S(1)} %add.122, f32[256,512]{1,0:T(8,128)S(1)} %add.122, f32[256,512]{1,0:T(8,128)S(1)} %add.122, f32[256,512]{1,0:T(8,128)S(1)} %add.122, ...), branch_computations={%region_7.8_spmd, %region_8.9_spmd, %region_9.10_spmd, %region_10.... | conditional | flops 262144 | bytes 2621488
  51.4 11.0 %collective-permute-start.11 = (bf16[256,512]{1,0:T(8,128)(2,1)S(1)}, bf16[256,512]{1,0:T(8,128)(2,1)S(1)}, u32[]{:S(2)}, u32[]{:S(2)}) collective-permute-start(bf16[256,512]{1,0:T(8,128)(2,1)S(1)} %convert_element_type.129), channel_id=1, source_target_pairs={{0,256},{256,0},{8,264},{264,8},{16,272},{272,16},{24,280},{280,24... | collective-permute-start | bytes 786440 | tf_op jit(solution)/shard_map/cond/branch_5_fun/ppermute | solution.py:29
  62.4 11.9 %collective-permute-done.11 = bf16[256,512]{1,0:T(8,128)(2,1)S(1)} collective-permute-done((bf16[256,512]{1,0:T(8,128)(2,1)S(1)}, bf16[256,512]{1,0:T(8,128)(2,1)S(1)}, u32[]{:S(2)}, u32[]{:S(2)}) %collective-permute-start.11) | collective-permute-done | bytes 262176 | tf_op jit(solution)/shard_map/cond/branch_5_fun/ppermute | solution.py:29
  74.4 1.0 %fusion.7 = bf16[1,256,512]{2,1,0:T(8,128)(2,1)} fusion(f32[256,512]{1,0:T(8,128)S(1)} %get-tuple-element.50, f32[256,512]{1,0:T(8,128)S(1)} %add.122, f32[256,512]{1,0:T(8,128)S(1)} %get-tuple-element.46, f32[256,512]{1,0:T(8,128)S(1)} %get-tuple-element.49, f32[256,512]{1,0:T(8,128)S(1)} %convert_add_fusion), kind=kLoop, calls=%fused_computation.17 | loop fusion | flops 917504 | bytes 2883584 | tf_op jit(solution)/shard_map/broadcast_in_dim | solution.py:104
  (26 shorter events, 0.4 us)
Async XLA Ops:
  0.0 15.8 %copy-start.4 = (s32[2]{0:T(128)S(1)}, s32[2]{0:T(128)}, u32[]{:S(2)}) copy-start(s32[2]{0:T(128)} %param.25) | copy-start | bytes 28
  0.0 18.3 %copy-start.3 = (s32[1,1,40]{2,1,0:T(1,128)S(1)}, s32[1,1,40]{2,1,0:T(1,128)}, u32[]{:S(2)}) copy-start(s32[1,1,40]{2,1,0:T(1,128)} %param.24) | copy-start | bytes 484
  1.7 26.7 %copy-start = (bf16[1,1024,512]{2,1,0:T(8,128)(2,1)S(1)}, bf16[1,1024,512]{2,1,0:T(8,128)(2,1)}, u32[]{:S(2)}) copy-start(bf16[1,1024,512]{2,1,0:T(8,128)(2,1)} %param.20) | copy-start | bytes 3145732
  1.7 26.7 %copy-start.1 = (bf16[1,256,512]{2,1,0:T(8,128)(2,1)S(1)}, bf16[1,256,512]{2,1,0:T(8,128)(2,1)}, u32[]{:S(2)}) copy-start(bf16[1,256,512]{2,1,0:T(8,128)(2,1)} %param.22) | copy-start | bytes 786436
  1.7 26.7 %copy-start.2 = (bf16[1,256,512]{2,1,0:T(8,128)(2,1)S(1)}, bf16[1,256,512]{2,1,0:T(8,128)(2,1)}, u32[]{:S(2)}) copy-start(bf16[1,256,512]{2,1,0:T(8,128)(2,1)} %param.21) | copy-start | bytes 786436
  1.7 26.7 %all-to-all-start = ((bf16[8,128,256]{2,1,0:T(8,128)(2,1)}), bf16[8,128,256]{2,1,0:T(8,128)(2,1)S(1)}, u32[]{:S(2)}, u32[]{:S(2)}) async-start(bf16[8,128,256]{2,1,0:T(8,128)(2,1)} %broadcast_in_dim.19), calls=%async_computation | async-start | bytes 1048576 | tf_op jit(solution)/shard_map/all_to_all | solution.py:35
  32.3 15.6 %collective-permute-start.2 = (bf16[256,512]{1,0:T(8,128)(2,1)S(1)}, bf16[256,512]{1,0:T(8,128)(2,1)S(1)}, u32[]{:S(2)}, u32[]{:S(2)}) collective-permute-start(bf16[256,512]{1,0:T(8,128)(2,1)S(1)} %convert_element_type.111), channel_id=1, source_target_pairs={{0,32},{32,0},{8,40},{40,8},{16,48},{48,16},{24,56},{56,24},{64,96... | collective-permute-start | bytes 786440 | tf_op jit(solution)/shard_map/cond/branch_2_fun/ppermute | solution.py:29
  51.4 22.9 %collective-permute-start.11 = (bf16[256,512]{1,0:T(8,128)(2,1)S(1)}, bf16[256,512]{1,0:T(8,128)(2,1)S(1)}, u32[]{:S(2)}, u32[]{:S(2)}) collective-permute-start(bf16[256,512]{1,0:T(8,128)(2,1)S(1)} %convert_element_type.129), channel_id=1, source_target_pairs={{0,256},{256,0},{8,264},{264,8},{16,272},{272,16},{24,280},{280,24... | collective-permute-start | bytes 786440 | tf_op jit(solution)/shard_map/cond/branch_5_fun/ppermute | solution.py:29

commit v2 on v0

v2 whole, which is shorter than its diff:
```python
import jax
import jax.numpy as jnp
import numpy as np
from jax import lax
from jax.experimental import pallas as pl
from jax.experimental.pallas import tpu as pltpu
from jax.sharding import PartitionSpec as P


learn_rate = 0.02
step = 0.25
ROWS, COLS, KEEP, SLABS = 256, 512, 40, 64
LEFT = SLABS - KEEP
f32, bf16, i32 = jnp.float32, jnp.bfloat16, jnp.int32
VM = pl.BlockSpec(memory_space=pltpu.VMEM)
SM = pl.BlockSpec(memory_space=pltpu.SMEM)


def tables():
    u, n = np.arange(64)[:, None], np.arange(64)[None, :]
    table = np.where(u == 0, np.sqrt(1 / 64), np.sqrt(2 / 64)) * np.cos(np.pi * (2 * n + 1) * u / 128)
    left = np.zeros((2, 8, 2, 8, 4, 64))
    for a in range(4):
        left[a // 2, :, a % 2, :, a, :] = table.reshape(8, 8, 64)
    left = left.reshape(ROWS, ROWS)
    right = np.zeros((8, 64, 8, 8, 8))
    for b in range(8):
        right[b, :, :, b, :] = table.T.reshape(64, 8, 8)
    right = right.reshape(COLS, COLS)

    def two(x):
        high = x.astype(jnp.bfloat16)
        return np.stack([high, (x - high.astype(np.float64)).astype(jnp.bfloat16)])

    return two(left), two(left.T), two(right), two(right.T)


def dot(a, b):
    return jnp.dot(a, b, preferred_element_type=f32)


def split(x):
    high = x.astype(bf16)
    return high, (x - high.astype(f32)).astype(bf16)


def left_dot(table, x):
    high, low = split(x)
    return dot(table[0], high) + (dot(table[0], low) + dot(table[1], high))


def right_dot(x, table):
    high, low = split(x)
    return dot(high, table[0]) + (dot(low, table[0]) + dot(high, table[1]))


def low_lanes():
    return lax.broadcasted_iota(i32, (128, 128), 1) < 64


def to_slabs(grid, put):
    low = low_lanes()
    for q in range(4):
        top = grid[:128, 128 * q : 128 * (q + 1)]
        bottom = grid[128:, 128 * q : 128 * (q + 1)]
        even = jnp.where(low, top, pltpu.roll(bottom, 64, 1))
        odd = jnp.where(low, pltpu.roll(top, 64, 1), bottom)
        for ub in range(8):
            put(ub * 8 + 2 * q, even[16 * ub : 16 * (ub + 1)])
            put(ub * 8 + 2 * q + 1, odd[16 * ub : 16 * (ub + 1)])


def from_slabs(get):
    low = low_lanes()
    tops, bottoms = [], []
    for q in range(4):
        even = jnp.concatenate([get(ub * 8 + 2 * q) for ub in range(8)], 0)
        odd = jnp.concatenate([get(ub * 8 + 2 * q + 1) for ub in range(8)], 0)
        tops.append(jnp.where(low, even, pltpu.roll(odd, 64, 1)))
        bottoms.append(jnp.where(low, pltpu.roll(even, 64, 1), odd))
    return jnp.concatenate([jnp.concatenate(tops, 1), jnp.concatenate(bottoms, 1)], 0)


def list_left(kept, rest):
    low, high = jnp.int32(0), jnp.int32(0)
    for i in range(KEEP):
        s = kept[i]
        bit = lax.shift_left(jnp.int32(1), s & 31)
        low = low | jnp.where(s < 32, bit, 0)
        high = high | jnp.where(s < 32, 0, bit)
    count = jnp.int32(0)
    for s in range(SLABS):
        rest[count] = s
        word = low if s < 32 else high
        count = count + 1 - (lax.shift_right_logical(word, jnp.int32(s & 31)) & 1)


def public_kernel(kept, public, kept_row, left, right, coeffs, early, rest):
    x = public[...]
    grid = left_dot(left, dot(x, right[0]) + dot(x, right[1]))

    def put(s, slab):
        coeffs[s] = slab

    to_slabs(grid, put)
    list_left(kept, rest)
    for j in range(LEFT):
        early[j] = coeffs[rest[j]].astype(bf16)
    early[LEFT] = kept_row[...]


def grads_kernel(count, place, grads, weight, left, right, turned, coeffs):
    def block(k, c):
        x = grads[pl.ds(pl.multiple_of(k * 256, 256), 256), :]
        y = dot(x, right[0]) + dot(x, right[1])
        token = k * 256 + lax.broadcasted_iota(i32, (256, COLS), 0)
        y = jnp.where(token < count[0], y, 0.0).astype(bf16)
        for z in range(2):
            to = k * 256 + lax.rem(z + place[0], 2) * 128
            turned[pl.ds(pl.multiple_of(to, 128), 128), :] = y[128 * z : 128 * (z + 1)]
        return c

    lax.fori_loop(0, grads.shape[0] // 256, block, 0)
    x = weight[...]
    coeffs[...] = left_dot(left, dot(x, right[0]) + dot(x, right[1]))


def weights_kernel(kept, acts, turned, weight_coeffs, left, after, late, kept_coeffs, moved, slabs):
    dims = (((1,), (1,)), ((), ()))
    x = acts[...].reshape(-1, ROWS)
    rows = lax.dot_general(left[0], x, dims, preferred_element_type=f32)
    rows += lax.dot_general(left[1], x, dims, preferred_element_type=f32)
    change = -learn_rate * dot(rows.astype(bf16), turned[...])
    moved[...] = change

    def put(s, slab):
        slabs[s] = slab

    to_slabs(weight_coeffs[...] + change, put)
    for i in range(KEEP):
        slab = slabs[kept[i]]
        kept_coeffs[i] = slab
        late[i] = slab.astype(bf16)


def fill_kernel(kept_peer, early, peer, rest):
    list_left(kept_peer, rest)
    for j in range(LEFT):
        peer[rest[j]] = early[j]
    for i in range(KEEP):
        peer[kept_peer[i]] = jnp.zeros((16, 128), bf16)


def first_kernel(kept, kept_peer, arrived, filled, kept_coeffs, late, next_coeffs, peer):
    peer[...] = filled[...]
    for i in range(KEEP):
        peer[kept_peer[i]] = arrived[i]
    for i in range(KEEP):
        value = kept_coeffs[i]
        value = value + step * (peer[kept[i]].astype(f32) - value)
        next_coeffs[i] = value
        late[i] = value.astype(bf16)


def base_kernel(kept, kept_peer, peer, early, coeffs, kept_coeffs, next_coeffs, moved, weight, left_t, right_t, out, delta, rest):
    list_left(kept_peer, rest)
    delta[...] = step * peer[...].astype(f32) - 2 * step * coeffs[...]
    for i in range(KEEP):
        s = kept[i]
        delta[s] = step * (peer[s].astype(f32) - kept_coeffs[i] - next_coeffs[i])
    for j in range(LEFT):
        s = rest[j]
        delta[s] = delta[s] + step * early[j].astype(f32)
    grid = from_slabs(lambda s: delta[s]) + moved[...]
    out[...] = weight[...].astype(f32) + left_dot(left_t, right_dot(grid, right_t))


def last_kernel(kept_peer, arrived, base, left_t, right_t, out, slabs):
    slabs[...] = jnp.zeros(slabs.shape, f32)

    for i in range(KEEP):
        slabs[kept_peer[i]] = step * arrived[i].astype(f32)
    grid = from_slabs(lambda s: slabs[s]).astype(bf16)
    change = dot(left_t[0], dot(grid, right_t[0]).astype(bf16))
    out[...] = (base[...] + change).astype(bf16)


def call(kernel, outs, specs, scratch=(), flops=0, moves=0):
    return pl.pallas_call(
        kernel,
        out_shape=[jax.ShapeDtypeStruct(shape, kind) for shape, kind in outs],
        in_specs=specs,
        out_specs=[VM] * len(outs),
        scratch_shapes=list(scratch),
        compiler_params=pltpu.CompilerParams(vmem_limit_bytes=32 * 2**20),
        cost_estimate=pl.CostEstimate(flops=flops, bytes_accessed=moves, transcendentals=0),
    )


SLAB32 = ((SLABS, 16, 128), f32)
SLAB16 = ((SLABS, 16, 128), bf16)
KEPT32 = ((KEEP, 16, 128), f32)
KEPT16 = ((KEEP, 16, 128), bf16)
GRID32 = ((ROWS, COLS), f32)
ANY = pl.BlockSpec(memory_space=pl.ANY)
REST = pltpu.SMEM((SLABS + 1,), i32)
ROOM = pltpu.VMEM((SLABS, 16, 128), f32)


def do_public(kept, public, kept_row, left, right):
    outs = [SLAB32, ((LEFT + 1, 16, 128), bf16)]
    return call(public_kernel, outs, [SM] + [VM] * 4, [REST], 10**9, 2**21)(kept, public, kept_row, left, right)


def do_grads(count, place, grads, weight, left, right):
    outs = [(grads.shape, bf16), GRID32]
    return call(grads_kernel, outs, [SM, SM] + [VM] * 4, (), 2 * 10**9, 2**22)(count, place, grads, weight, left, right)


def do_weights(kept, acts, turned, weight_coeffs, left, after):
    outs = [KEPT16, KEPT32, GRID32]
    return call(weights_kernel, outs, [SM] + [VM] * 4 + [ANY], [ROOM], 3 * 10**8, 2**21)(kept, acts, turned, weight_coeffs, left, after)


def do_fill(kept_peer, early):
    return call(fill_kernel, [SLAB16], [SM, VM], [REST], 10**6, 2**18)(kept_peer, early)[0]


def do_first(kept, kept_peer, arrived, filled, kept_coeffs):
    return call(first_kernel, [KEPT16, KEPT32, SLAB16], [SM, SM] + [VM] * 3, (), 10**6, 2**19)(kept, kept_peer, arrived, filled, kept_coeffs)


def do_base(kept, kept_peer, *rest):
    return call(base_kernel, [GRID32], [SM, SM] + [VM] * 9, [ROOM, REST], 10**9, 2**22)(kept, kept_peer, *rest)[0]


def do_last(kept_peer, arrived, base, left_t, right_t):
    outs = [((ROWS, COLS), bf16)]
    return call(last_kernel, outs, [SM] + [VM] * 4, [ROOM], 2 * 10**8, 2**20)(kept_peer, arrived, base, left_t, right_t)[0]


def swapped(block, axis, bit):
    count = lax.axis_size(axis)
    return lax.ppermute(block, axis, [(i, i ^ (1 << bit)) for i in range(count)])


def peers_list(early):
    return early[LEFT, 0, :KEEP].astype(i32)


def window(bits, pair, turned, weight_coeffs, weight, public, kept, left, left_t, right, right_t):
    count_x = lax.axis_size("tp") // 2
    groups = [[2 * x + z for x in range(count_x)] for z in range(2)]
    kept_row = jnp.pad(kept.astype(bf16)[None], ((0, 15), (0, 128 - KEEP)))
    acts = lax.all_to_all(jnp.broadcast_to(pair[None], (count_x,) + pair.shape), "tp", 0, 0, axis_index_groups=groups)
    coeffs, early = do_public(kept, public, kept_row, left, right)
    early_first = swapped(early, "rep", bits[0])
    late, kept_coeffs, moved = do_weights(kept, acts, turned, weight_coeffs, left, early)
    arrived = swapped(late, "rep", bits[0])
    early, late = lax.optimization_barrier((early, late))
    early_second = swapped(early, "rep", bits[1])
    kept_first, kept_second = peers_list(early_first), peers_list(early_second)
    filled = do_fill(kept_first, early_first)
    late, next_coeffs, peer = do_first(kept, kept_first, arrived, filled, kept_coeffs)
    arrived = swapped(late, "rep", bits[1])
    base = do_base(kept, kept_second, peer, early_second, coeffs, kept_coeffs, next_coeffs, moved, weight, left_t, right_t)
    return do_last(kept_second, arrived, base, left_t, right_t)


def shards(activations, out_grads, weight, public, counts, kept, distances):
    acts = activations[0]
    other = swapped(acts, "tp", 0)
    top = lax.axis_size("rep").bit_length() - 2
    bits = lax.population_count(distances - 1)
    choice = jnp.where(bits[1] == top, bits[0], top + bits[1])
    ways = [(k, top) for k in range(top)] + [(top, k) for k in range(top)]
    place = (lax.axis_index("tp") % 2).astype(i32)[None]
    left, left_t, right, right_t = (jnp.asarray(t) for t in tables())
    turned, weight_coeffs = do_grads(counts, place, out_grads[0], weight[0], left, right)
    operands = (jnp.stack([acts, other]), turned, weight_coeffs, weight[0], public[0], kept[0, 0], left, left_t, right, right_t)
    branches = [lambda *args, way=way: window(way, *args) for way in ways]
    return lax.switch(choice, branches, *operands)[None]


def solution(mesh):
    return jax.shard_map(
        shards,
        mesh=mesh,
        in_specs=(
            P("rep", "tp", None),
            P("rep", None, "tp"),
            P("rep", None, "tp"),
            P("rep", None, "tp"),
            P("rep"),
            P("rep", "tp", None),
            P(),
        ),
        out_specs=P("rep", None, "tp"),
        check_vma=False,
    )
```

time: 97.6 us -> 60.2 us (0.62)
  the two profiles are of different devices: /device:TPU:40 before, /device:TPU:1 now
where the time goes in v2:
time: 60.2 us; the launch traced here: 59.8 us
  starting transfers between devices  29.3 us (49%)
  Pallas kernels  12.1 us (20%)
  waiting for transfers between devices  10.3 us (17%)
  local copies, waits for them, and re-layouts  4.69 us (8%)
  between operations  2.68 us (4%)
  loops' own time  0.65 us (1%)
    ppermute x5, starting transfers between devices, swapped(): return lax.ppermute(block, axis, [(i, i ^ 1 << bit) for i in range(count)])  25.3 us
    ppermute x5, waiting for transfers between devices, swapped(): return lax.ppermute(block, axis, [(i, i ^ 1 << bit) for i in range(count)])  7.71 us
    all_to_all x1, starting transfers between devices, window(): lax.all_to_all(jnp.broadcast_to(pair[None], (count_x,) + pair.shape), 'tp...  4.02 us
    pallas_call x1, Pallas kernels, do_grads(): call(grads_kernel, outs, [SM, SM] + [VM] * 4, (), 2 * 10 ** 9, 2 ** 22)  3.96 us
    unnamed x16, local copies, waits for them, and re-layouts  3.2 us
    all_to_all x1, waiting for transfers between devices, window(): lax.all_to_all(jnp.broadcast_to(pair[None], (count_x,) + pair.shape), 'tp...  2.59 us
    pallas_call x1, Pallas kernels, do_public(): call(public_kernel, outs, [SM] + [VM] * 4, [REST], 10 ** 9, 2 ** 21)  2.24 us
    pallas_call x1, Pallas kernels, do_base(): call(base_kernel, [GRID32], [SM, SM] + [VM] * 9, [ROOM, REST], 10 ** 9, 2...  1.91 us
  transfers between devices with their start and end apart: 6, of which 3 were waited for; matrix products, arithmetic and copies ran while one was open for 1% of the time, Pallas kernels for 18%

profile of v2, /device:TPU:1, one launch (start us, length us, event | category | flops | bytes accessed | tf_op | source)
XLA Modules:
  0.0 59.8 jit_solution(17606259112809933582)
XLA Ops:
  0.0 11.5 %collective-permute-start.40 = (bf16[128,256]{1,0:T(8,128)(2,1)}, bf16[128,256]{1,0:T(8,128)(2,1)S(1)}, u32[]{:S(2)}, u32[]{:S(2)}) collective-permute-start(bf16[128,256]{1,0:T(8,128)(2,1)} %bitcast.218), channel_id=1, source_target_pairs={{0,1},{1,0},{2,3},{3,2},{4,5},{5,4},{6,7},{7,6},{8,9},{9,8},{10,11... | collective-permute-start | bytes 196616 | tf_op jit(solution)/shard_map/ppermute | solution.py:244
  11.5 0.6 %copy-done.27 = s32[2]{0:T(128)S(1)} copy-done((s32[2]{0:T(128)S(1)}, s32[2]{0:T(128)}, u32[]{:S(2)}) %copy-start.27) | copy-done | bytes 32
  12.8 0.0 copy-start.20
  12.8 1.2 %copy-done.20 = bf16[1,1024,512]{2,1,0:T(8,128)(2,1)S(1)} copy-done((bf16[1,1024,512]{2,1,0:T(8,128)(2,1)S(1)}, bf16[1,1024,512]{2,1,0:T(8,128)(2,1)}, u32[]{:S(2)}) %copy-start.20) | copy-done | bytes 1048600
  14.0 4.0 %shard_map.159 = (bf16[1024,512]{1,0:T(8,128)(2,1)S(1)}, f32[256,512]{1,0:T(8,128)S(1)}) custom-call(s32[1]{0:T(128)S(6)} %copy.72.count, s32[1]{0:T(128)} %bitcast.83.place, bf16[1024,512]{1,0:T(8,128)(2,1)S(1)} %bitcast.156, bf16[256,512]{1,0:T(8,128)(2,1)} %bitcast.157, bf16[2,256,256]{2,1,0:T(8,128)(2,1)} %constant.68.clone.left, ...), custom_call_target="tpu_custom_call" | custom-call | flops 2000000000 | bytes 4194304 | tf_op jit(solution)/shard_map/pallas_call | solution.py:217
  18.0 0.0 copy-start.21
  18.0 0.6 %fusion.20 = (s32[1]{0:T(128)}, s32[1]{0:T(128)}) fusion(s32[2]{0:T(128)S(1)} %add_popcnt_fusion), kind=kLoop, calls=%fused_computation.52 | loop fusion | bytes 16 | tf_op jit(solution)/shard_map/slice | solution.py:275
  20.5 0.0 collective-permute-done.40
  20.6 0.0 copy-start.23
  20.6 0.6 %copy-done.23 = s32[1,1,40]{2,1,0:T(1,128)S(1)} copy-done((s32[1,1,40]{2,1,0:T(1,128)S(1)}, s32[1,1,40]{2,1,0:T(1,128)}, u32[]{:S(2)}) %copy-start.23) | copy-done | bytes 184
  21.2 37.8 %conditional.1 = (bf16[1,256,512]{2,1,0:T(8,128)(2,1)S(1)}) conditional(s32[]{:T(128)} %bitcast.80, (s32[1,1,40]{2,1,0:T(1,128)S(1)}, bf16[1,256,512]{2,1,0:T(8,128)(2,1)S(1)}, bf16[2,256,256]{2,1,0:T(8,128)(2,1)S(1)}, bf16[2,512,512]{2,1,0:T(8,128)(2,1)}, bf16[2,128,256]{2,1,0:T(8,128)(2,1)S(1)}, ...), branch_computations={%region_0.1_spmd, %region_1.2_spmd, %region_2.3_spmd, %region_3.4_... | conditional | flops 2502000128 | bytes 19829794 | solution.py:282
  21.2 0.8 %broadcast_in_dim.61 = bf16[4,2,128,256]{3,2,1,0:T(8,128)(2,1)} broadcast(bf16[2,128,256]{2,1,0:T(8,128)(2,1)S(1)} %get-tuple-element.242), dimensions={1,2,3} | broadcast | bytes 655360 | tf_op jit(solution)/shard_map/cond/branch_0_fun/broadcast_in_dim | solution.py:255
  22.1 4.0 %all-to-all-start = ((bf16[4,2,128,256]{3,2,1,0:T(8,128)(2,1)}), bf16[4,2,128,256]{3,2,1,0:T(8,128)(2,1)S(1)}, u32[]{:S(2)}, u32[]{:S(2)}) async-start(bf16[4,2,128,256]{3,2,1,0:T(8,128)(2,1)} %broadcast_in_dim.61), calls=%async_computation | async-start | bytes 1048576 | tf_op jit(solution)/shard_map/cond/branch_0_fun/all_to_all | solution.py:255
  26.1 2.2 %branch_0_fun.6 = (f32[64,16,128]{2,1,0:T(8,128)S(1)}, bf16[25,16,128]{2,1,0:T(8,128)(2,1)S(1)}) custom-call(s32[40]{0:T(128)S(1)} %bitcast.168, bf16[256,512]{1,0:T(8,128)(2,1)S(1)} %bitcast.220, bf16[16,128]{1,0:T(8,128)(2,1)S(1)} %pad.21.kept_row, bf16[2,256,256]{2,1,0:T(8,128)(2,1)S(1)} %get-tuple-element.239.left, ...), custom_call_target="tpu_custom_call" | custom-call | flops 1000000000 | bytes 2097152 | tf_op jit(solution)/shard_map/cond/branch_0_fun/pallas_call | solution.py:212
  28.4 3.1 %collective-permute-start.1 = (bf16[25,16,128]{2,1,0:T(8,128)(2,1)S(1)}, bf16[25,16,128]{2,1,0:T(8,128)(2,1)S(1)}, u32[]{:S(2)}, u32[]{:S(2)}) collective-permute-start(bf16[25,16,128]{2,1,0:T(8,128)(2,1)S(1)} %get-tuple-element.246.after), channel_id=1, source_target_pairs={{0,8},{8,0},{16,24},{24,16},{32,40},{40,32},{48,56},{56,48},{64,72... | collective-permute-start | bytes 307208 | tf_op jit(solution)/shard_map/cond/branch_0_fun/ppermute | solution.py:244
  31.5 2.6 %all-to-all-done.acts = bf16[4,2,128,256]{3,2,1,0:T(8,128)(2,1)S(1)} async-done(((bf16[4,2,128,256]{3,2,1,0:T(8,128)(2,1)}), bf16[4,2,128,256]{3,2,1,0:T(8,128)(2,1)S(1)}, u32[]{:S(2)}, u32[]{:S(2)}) %all-to-all-start) | async-done | bytes 524320 | tf_op jit(solution)/shard_map/cond/branch_0_fun/all_to_all | solution.py:255
  34.1 1.5 %branch_0_fun.7 = (bf16[40,16,128]{2,1,0:T(8,128)(2,1)S(1)}, f32[40,16,128]{2,1,0:T(8,128)S(1)}, f32[256,512]{1,0:T(8,128)S(1)}) custom-call(s32[40]{0:T(128)S(1)} %bitcast.169, bf16[4,2,128,256]{3,2,1,0:T(8,128)(2,1)S(1)} %all-to-all-done.acts, bf16[1024,512]{1,0:T(8,128)(2,1)S(1)} %get-tuple-element.243.turned, ...), custom_call_target="tpu_custom_call" | custom-call | flops 300000000 | bytes 2097152 | tf_op jit(solution)/shard_map/cond/branch_0_fun/pallas_call | solution.py:222
  35.5 0.0 copy-start
  35.6 4.5 %collective-permute-start.2 = (bf16[40,16,128]{2,1,0:T(8,128)(2,1)S(1)}, bf16[40,16,128]{2,1,0:T(8,128)(2,1)S(1)}, u32[]{:S(2)}, u32[]{:S(2)}) collective-permute-start(bf16[40,16,128]{2,1,0:T(8,128)(2,1)S(1)} %get-tuple-element.245), channel_id=1, source_target_pairs={{0,8},{8,0},{16,24},{24,16},{32,40},{40,32},{48,56},{56,48},{64,72... | collective-permute-start | bytes 491528 | tf_op jit(solution)/shard_map/cond/branch_0_fun/ppermute | solution.py:244
  40.1 4.0 %collective-permute-start = (bf16[25,16,128]{2,1,0:T(8,128)(2,1)S(1)}, bf16[25,16,128]{2,1,0:T(8,128)(2,1)S(1)}, u32[]{:S(2)}, u32[]{:S(2)}) collective-permute-start(bf16[25,16,128]{2,1,0:T(8,128)(2,1)S(1)} %get-tuple-element.246.after), channel_id=1, source_target_pairs={{0,256},{8,264},{16,272},{24,280},{32,288},{40,296},{48,304},{56,3... | collective-permute-start | bytes 307208 | tf_op jit(solution)/shard_map/cond/branch_0_fun/ppermute | solution.py:244
  44.1 0.0 collective-permute-done.1.early
  44.1 0.8 %branch_0_fun.8.filled = bf16[64,16,128]{2,1,0:T(8,128)(2,1)S(1)} custom-call(s32[40]{0:T(128)S(1)} %fusion.kept_peer, bf16[25,16,128]{2,1,0:T(8,128)(2,1)S(1)} %collective-permute-done.1.early), custom_call_target="tpu_custom_call" | custom-call | flops 1000000 | bytes 262144 | tf_op jit(solution)/shard_map/cond/branch_0_fun/pallas_call | solution.py:226
  44.9 0.0 collective-permute-done.2.arrived
  44.9 0.6 %branch_0_fun.9 = (bf16[40,16,128]{2,1,0:T(8,128)(2,1)S(1)}, f32[40,16,128]{2,1,0:T(8,128)S(1)}, bf16[64,16,128]{2,1,0:T(8,128)(2,1)S(1)}) custom-call(s32[40]{0:T(128)S(1)} %bitcast.170, s32[40]{0:T(128)S(1)} %fusion.kept_peer, bf16[40,16,128]{2,1,0:T(8,128)(2,1)S(1)} %collective-permute-done.2.arrived, bf16[64,16,128]{2,1,0:T(8,128)(2,1)S(1)} %branch_0_fun.8.filled, ...), custom_call_target="tpu_custom_call" | custom-call | flops 1000000 | bytes 524288 | tf_op jit(solution)/shard_map/cond/branch_0_fun/pallas_call | solution.py:230
  45.6 2.2 %collective-permute-start.3 = (bf16[40,16,128]{2,1,0:T(8,128)(2,1)S(1)}, bf16[40,16,128]{2,1,0:T(8,128)(2,1)S(1)}, u32[]{:S(2)}, u32[]{:S(2)}) collective-permute-start(bf16[40,16,128]{2,1,0:T(8,128)(2,1)S(1)} %get-tuple-element.248), channel_id=1, source_target_pairs={{0,256},{8,264},{16,272},{24,280},{32,288},{40,296},{48,304},{56,3... | collective-permute-start | bytes 491528 | tf_op jit(solution)/shard_map/cond/branch_0_fun/ppermute | solution.py:244
  47.7 1.8 %collective-permute-done.early = bf16[25,16,128]{2,1,0:T(8,128)(2,1)S(1)} collective-permute-done((bf16[25,16,128]{2,1,0:T(8,128)(2,1)S(1)}, bf16[25,16,128]{2,1,0:T(8,128)(2,1)S(1)}, u32[]{:S(2)}, u32[]{:S(2)}) %collective-permute-start) | collective-permute-done | bytes 102432 | tf_op jit(solution)/shard_map/cond/branch_0_fun/ppermute | solution.py:244
  49.5 0.0 copy-done.10
  49.6 1.9 %branch_0_fun.10.base = f32[256,512]{1,0:T(8,128)S(1)} custom-call(s32[40]{0:T(128)S(1)} %bitcast.171, s32[40]{0:T(128)S(1)} %fusion.1.kept_peer, bf16[64,16,128]{2,1,0:T(8,128)(2,1)S(1)} %get-tuple-element.249.peer, bf16[25,16,128]{2,1,0:T(8,128)(2,1)S(1)} %collective-permute-done.early, f32[64,16,128]{2,1,0:T(8,128)S(1)} %get-tuple-element.250.coeffs, ...), custom_call_target="tpu_custom_call" | custom-call | flops 1000000000 | bytes 4194304 | tf_op jit(solution)/shard_map/cond/branch_0_fun/pallas_call | solution.py:234
  51.5 5.9 %collective-permute-done.3.arrived = bf16[40,16,128]{2,1,0:T(8,128)(2,1)S(1)} collective-permute-done((bf16[40,16,128]{2,1,0:T(8,128)(2,1)S(1)}, bf16[40,16,128]{2,1,0:T(8,128)(2,1)S(1)}, u32[]{:S(2)}, u32[]{:S(2)}) %collective-permute-start.3) | collective-permute-done | bytes 163872 | tf_op jit(solution)/shard_map/cond/branch_0_fun/ppermute | solution.py:244
  57.4 1.1 %branch_0_fun.11 = bf16[256,512]{1,0:T(8,128)(2,1)S(1)} custom-call(s32[40]{0:T(128)S(1)} %fusion.1.kept_peer, bf16[40,16,128]{2,1,0:T(8,128)(2,1)S(1)} %collective-permute-done.3.arrived, f32[256,512]{1,0:T(8,128)S(1)} %branch_0_fun.10.base, bf16[2,256,256]{2,1,0:T(8,128)(2,1)S(1)} %copy-done.10, bf16[2,512,512]{2,1,0:T(8,128)(2,1)S(1)} %copy-done), custom_call_target="tpu_custom_call" | custom-call | flops 200000000 | bytes 1048576 | tf_op jit(solution)/shard_map/cond/branch_0_fun/pallas_call | solution.py:239
  59.1 0.0 copy-start.24
  59.1 0.7 %copy-done.24 = bf16[1,256,512]{2,1,0:T(8,128)(2,1)} copy-done((bf16[1,256,512]{2,1,0:T(8,128)(2,1)}, bf16[1,256,512]{2,1,0:T(8,128)(2,1)S(1)}, u32[]{:S(2)}) %copy-start.24) | copy-done | bytes 262168
  (16 shorter events, 0.1 us)
Async XLA Ops:
  0.0 20.5 %collective-permute-start.40 = (bf16[128,256]{1,0:T(8,128)(2,1)}, bf16[128,256]{1,0:T(8,128)(2,1)S(1)}, u32[]{:S(2)}, u32[]{:S(2)}) collective-permute-start(bf16[128,256]{1,0:T(8,128)(2,1)} %bitcast.218), channel_id=1, source_target_pairs={{0,1},{1,0},{2,3},{3,2},{4,5},{5,4},{6,7},{7,6},{8,9},{9,8},{10,11... | collective-permute-start | bytes 196616 | tf_op jit(solution)/shard_map/ppermute | solution.py:244
  11.5 0.7 %copy-start.27 = (s32[2]{0:T(128)S(1)}, s32[2]{0:T(128)}, u32[]{:S(2)}) copy-start(s32[2]{0:T(128)} %param.27) | copy-start | bytes 28
  12.8 1.2 %copy-start.20 = (bf16[1,1024,512]{2,1,0:T(8,128)(2,1)S(1)}, bf16[1,1024,512]{2,1,0:T(8,128)(2,1)}, u32[]{:S(2)}) copy-start(bf16[1,1024,512]{2,1,0:T(8,128)(2,1)} %param.22) | copy-start | bytes 3145732
  14.0 6.5 %copy-start.25 = (bf16[1,128,256]{2,1,0:T(8,128)(2,1)S(1)}, bf16[1,128,256]{2,1,0:T(8,128)(2,1)}, u32[]{:S(2)}) copy-start(bf16[1,128,256]{2,1,0:T(8,128)(2,1)} %param.21) | copy-start | bytes 196612
  14.0 6.6 %copy-start.22 = (bf16[1,256,512]{2,1,0:T(8,128)(2,1)S(1)}, bf16[1,256,512]{2,1,0:T(8,128)(2,1)}, u32[]{:S(2)}) copy-start(bf16[1,256,512]{2,1,0:T(8,128)(2,1)} %param.23) | copy-start | bytes 786436
  14.0 6.6 %copy-start.26 = (bf16[1,256,512]{2,1,0:T(8,128)(2,1)S(1)}, bf16[1,256,512]{2,1,0:T(8,128)(2,1)}, u32[]{:S(2)}) copy-start(bf16[1,256,512]{2,1,0:T(8,128)(2,1)} %param.24) | copy-start | bytes 786436
  18.0 2.6 %copy-start.21 = (bf16[2,256,256]{2,1,0:T(8,128)(2,1)S(1)}, bf16[2,256,256]{2,1,0:T(8,128)(2,1)}, u32[]{:S(2)}) copy-start(bf16[2,256,256]{2,1,0:T(8,128)(2,1)} %constant.68.clone.left) | copy-start | bytes 786436
  20.6 0.7 %copy-start.23 = (s32[1,1,40]{2,1,0:T(1,128)S(1)}, s32[1,1,40]{2,1,0:T(1,128)}, u32[]{:S(2)}) copy-start(s32[1,1,40]{2,1,0:T(1,128)} %param.26) | copy-start | bytes 484
  22.1 12.0 %all-to-all-start = ((bf16[4,2,128,256]{3,2,1,0:T(8,128)(2,1)}), bf16[4,2,128,256]{3,2,1,0:T(8,128)(2,1)S(1)}, u32[]{:S(2)}, u32[]{:S(2)}) async-start(bf16[4,2,128,256]{3,2,1,0:T(8,128)(2,1)} %broadcast_in_dim.61), calls=%async_computation | async-start | bytes 1048576 | tf_op jit(solution)/shard_map/cond/branch_0_fun/all_to_all | solution.py:255
  28.4 15.7 %collective-permute-start.1 = (bf16[25,16,128]{2,1,0:T(8,128)(2,1)S(1)}, bf16[25,16,128]{2,1,0:T(8,128)(2,1)S(1)}, u32[]{:S(2)}, u32[]{:S(2)}) collective-permute-start(bf16[25,16,128]{2,1,0:T(8,128)(2,1)S(1)} %get-tuple-element.246.after), channel_id=1, source_target_pairs={{0,8},{8,0},{16,24},{24,16},{32,40},{40,32},{48,56},{56,48},{64,72... | collective-permute-start | bytes 307208 | tf_op jit(solution)/shard_map/cond/branch_0_fun/ppermute | solution.py:244
  34.1 15.5 %copy-start.10 = (bf16[2,256,256]{2,1,0:T(8,128)(2,1)S(1)}, bf16[2,256,256]{2,1,0:T(8,128)(2,1)}, u32[]{:S(2)}) copy-start(bf16[2,256,256]{2,1,0:T(8,128)(2,1)} %constant.69.clone.1.left_t) | copy-start | bytes 786436 | tf_op jit(solution)/shard_map/cond
  35.5 14.0 %copy-start = (bf16[2,512,512]{2,1,0:T(8,128)(2,1)S(1)}, bf16[2,512,512]{2,1,0:T(8,128)(2,1)}, u32[]{:S(2)}) copy-start(bf16[2,512,512]{2,1,0:T(8,128)(2,1)} %constant.71.clone.1.right_t) | copy-start | bytes 3145732 | tf_op jit(solution)/shard_map/cond
  35.6 9.4 %collective-permute-start.2 = (bf16[40,16,128]{2,1,0:T(8,128)(2,1)S(1)}, bf16[40,16,128]{2,1,0:T(8,128)(2,1)S(1)}, u32[]{:S(2)}, u32[]{:S(2)}) collective-permute-start(bf16[40,16,128]{2,1,0:T(8,128)(2,1)S(1)} %get-tuple-element.245), channel_id=1, source_target_pairs={{0,8},{8,0},{16,24},{24,16},{32,40},{40,32},{48,56},{56,48},{64,72... | collective-permute-start | bytes 491528 | tf_op jit(solution)/shard_map/cond/branch_0_fun/ppermute | solution.py:244
  40.1 9.5 %collective-permute-start = (bf16[25,16,128]{2,1,0:T(8,128)(2,1)S(1)}, bf16[25,16,128]{2,1,0:T(8,128)(2,1)S(1)}, u32[]{:S(2)}, u32[]{:S(2)}) collective-permute-start(bf16[25,16,128]{2,1,0:T(8,128)(2,1)S(1)} %get-tuple-element.246.after), channel_id=1, source_target_pairs={{0,256},{8,264},{16,272},{24,280},{32,288},{40,296},{48,304},{56,3... | collective-permute-start | bytes 307208 | tf_op jit(solution)/shard_map/cond/branch_0_fun/ppermute | solution.py:244
  45.6 11.8 %collective-permute-start.3 = (bf16[40,16,128]{2,1,0:T(8,128)(2,1)S(1)}, bf16[40,16,128]{2,1,0:T(8,128)(2,1)S(1)}, u32[]{:S(2)}, u32[]{:S(2)}) collective-permute-start(bf16[40,16,128]{2,1,0:T(8,128)(2,1)S(1)} %get-tuple-element.248), channel_id=1, source_target_pairs={{0,256},{8,264},{16,272},{24,280},{32,288},{40,296},{48,304},{56,3... | collective-permute-start | bytes 491528 | tf_op jit(solution)/shard_map/cond/branch_0_fun/ppermute | solution.py:244
  59.1 0.7 %copy-start.24 = (bf16[1,256,512]{2,1,0:T(8,128)(2,1)}, bf16[1,256,512]{2,1,0:T(8,128)(2,1)S(1)}, u32[]{:S(2)}) copy-start(bf16[1,256,512]{2,1,0:T(8,128)(2,1)S(1)} %get-tuple-element.614) | copy-start | bytes 786436

commit v3 on v2

v3 whole, which is shorter than its diff:
```python
import jax
import jax.numpy as jnp
import numpy as np
from jax import lax
from jax.experimental import pallas as pl
from jax.experimental.pallas import tpu as pltpu
from jax.sharding import PartitionSpec as P


learn_rate = 0.02
step = 0.25
ROWS, COLS, KEEP, SLABS = 256, 512, 40, 64
LEFT = SLABS - KEEP
f32, bf16, i32 = jnp.float32, jnp.bfloat16, jnp.int32
VM = pl.BlockSpec(memory_space=pltpu.VMEM)
SM = pl.BlockSpec(memory_space=pltpu.SMEM)


def cosines(freq, place):
    phase = ((2 * place + 1) * freq) & 255
    scale = jnp.where(freq == 0, np.float32(np.sqrt(1 / 64)), np.float32(np.sqrt(2 / 64)))
    return scale * jnp.cos(phase.astype(f32) * np.float32(np.pi / 128))


def lines(shape, axis):
    return lax.broadcasted_iota(i32, shape, axis)


def row_freq(r):
    return ((r >> 4) & 7) * 8 + (r & 7)


def row_tile(r):
    return 2 * (r >> 7) + ((r >> 3) & 1)


def col_freq(j):
    return (j >> 6) * 8 + (j & 7)


def col_tile(j):
    return (j >> 3) & 7


def left_table():
    shape = (ROWS, 128)
    part = cosines(row_freq(lines(shape, 0)), lines(shape, 1) & 63)
    shape = (ROWS, ROWS)
    return jnp.where(row_tile(lines(shape, 0)) == lines(shape, 1) >> 6, jnp.concatenate([part] * 2, 1), 0.0)


def left_table_t():
    shape = (64, ROWS)
    part = cosines(row_freq(lines(shape, 1)), lines(shape, 0))
    shape = (ROWS, ROWS)
    return jnp.where(row_tile(lines(shape, 1)) == lines(shape, 0) >> 6, jnp.concatenate([part] * 4, 0), 0.0)


def right_table():
    shape = (64, COLS)
    part = cosines(col_freq(lines(shape, 1)), lines(shape, 0))
    shape = (COLS, COLS)
    return jnp.where(col_tile(lines(shape, 1)) == lines(shape, 0) >> 6, jnp.concatenate([part] * 8, 0), 0.0)


def right_table_t():
    shape = (COLS, 128)
    part = cosines(col_freq(lines(shape, 0)), lines(shape, 1) & 63)
    shape = (COLS, COLS)
    return jnp.where(col_tile(lines(shape, 0)) == lines(shape, 1) >> 6, jnp.concatenate([part] * 4, 1), 0.0)


def dot(a, b):
    return jnp.dot(a, b, preferred_element_type=f32)


def split(x):
    high = x.astype(bf16)
    return high, (x - high.astype(f32)).astype(bf16)


def left_dot(table, x):
    high, low = split(x)
    return dot(table[0], high) + (dot(table[0], low) + dot(table[1], high))


def right_dot(x, table):
    high, low = split(x)
    return dot(high, table[0]) + (dot(low, table[0]) + dot(high, table[1]))


def low_lanes():
    return lax.broadcasted_iota(i32, (128, 128), 1) < 64


def to_slabs(grid, put):
    low = low_lanes()
    for q in range(4):
        top = grid[:128, 128 * q : 128 * (q + 1)]
        bottom = grid[128:, 128 * q : 128 * (q + 1)]
        even = jnp.where(low, top, pltpu.roll(bottom, 64, 1))
        odd = jnp.where(low, pltpu.roll(top, 64, 1), bottom)
        for ub in range(8):
            put(ub * 8 + 2 * q, even[16 * ub : 16 * (ub + 1)])
            put(ub * 8 + 2 * q + 1, odd[16 * ub : 16 * (ub + 1)])


def from_slabs(get):
    low = low_lanes()
    tops, bottoms = [], []
    for q in range(4):
        even = jnp.concatenate([get(ub * 8 + 2 * q) for ub in range(8)], 0)
        odd = jnp.concatenate([get(ub * 8 + 2 * q + 1) for ub in range(8)], 0)
        tops.append(jnp.where(low, even, pltpu.roll(odd, 64, 1)))
        bottoms.append(jnp.where(low, pltpu.roll(even, 64, 1), odd))
    return jnp.concatenate([jnp.concatenate(tops, 1), jnp.concatenate(bottoms, 1)], 0)


def list_all(kept, rest):
    lane = lax.broadcasted_iota(i32, (16, 128), 1)
    row = jnp.zeros((16, 128), f32)
    low, high = jnp.int32(0), jnp.int32(0)
    for i in range(KEEP):
        s = kept[i]
        row = jnp.where(lane == i, s.astype(f32), row)
        bit = lax.shift_left(jnp.int32(1), s & 31)
        low = low | jnp.where(s < 32, bit, 0)
        high = high | jnp.where(s < 32, 0, bit)
    count = jnp.int32(0)
    for s in range(SLABS):
        rest[count] = s
        row = jnp.where(lane == count + KEEP, jnp.float32(s), row)
        word = low if s < 32 else high
        count = count + 1 - (lax.shift_right_logical(word, jnp.int32(s & 31)) & 1)
    return row


def public_kernel(kept, public, coeffs, full, early, left_two, right_two, rest):
    left, right = split(left_table()), split(right_table())
    for k in range(2):
        left_two[k] = left[k]
        right_two[k] = right[k]
    x = public[...]
    grid = left_dot(left_two, dot(x, right_two[0]) + dot(x, right_two[1]))

    def put(s, slab):
        coeffs[s] = slab
        full[s] = slab.astype(bf16)

    to_slabs(grid, put)
    row = list_all(kept, rest)
    for j in range(LEFT):
        early[j] = full[rest[j]]
    early[LEFT] = row.astype(bf16)


def spread_kernel(own, other, out):
    for x in range(out.shape[0]):
        out[x, 0] = own[...]
        out[x, 1] = other[...]


def grads_kernel(count, place, way, grads, weight, right, turned, weight_turned):
    part = grads.shape[0] // 4
    for k in range(4):
        y = dot(grads[k * part : (k + 1) * part], right[0])
        token = k * part + lines((part, COLS), 0)
        y = jnp.where(token < count[0], y, 0.0).astype(bf16)
        for z in range(2):
            to = k * part + ((z + place[0]) & 1) * (part // 2)
            turned[pl.ds(pl.multiple_of(to, part // 2), part // 2), :] = y[part // 2 * z : part // 2 * (z + 1)]
    x = weight[...]
    weight_turned[...] = (dot(x, right[0]) + dot(x, right[1])).astype(bf16)


def weights_kernel(kept, acts, turned, weight_turned, left, public_full, packed, full, kept_coeffs, moved, slabs):
    dims = (((1,), (1,)), ((), ()))
    x = acts[...].reshape(-1, ROWS)
    rows = lax.dot_general(left[0], x, dims, preferred_element_type=f32)
    rows += lax.dot_general(left[1], x, dims, preferred_element_type=f32)
    change = -learn_rate * dot(rows.astype(bf16), turned[...])
    moved[...] = change

    def put(s, slab):
        slabs[s] = slab

    x = weight_turned[...]
    to_slabs(dot(left[0], x) + dot(left[1], x) + change, put)
    full[...] = public_full[...]
    for i in range(KEEP):
        s = kept[i]
        slab = slabs[s]
        short = slab.astype(bf16)
        kept_coeffs[i] = slab
        packed[i] = short
        full[s] = short


def fill_kernel(listed, early, peer):
    for j in range(LEFT):
        peer[listed[KEEP + j]] = early[j]
    for i in range(KEEP):
        peer[listed[i]] = jnp.zeros((16, 128), bf16)


def mix(kept, peer, own, kept_coeffs, packed, full, next_coeffs):
    full[...] = own[...]
    for i in range(KEEP):
        s = kept[i]
        value = kept_coeffs[i]
        value = value + step * (peer[s].astype(f32) - value)
        short = value.astype(bf16)
        next_coeffs[i] = value
        packed[i] = short
        full[s] = short


def near_kernel(kept, peer, own, kept_coeffs, packed, full, next_coeffs):
    mix(kept, peer, own, kept_coeffs, packed, full, next_coeffs)


def far_kernel(kept, listed, arrived, filled, own, kept_coeffs, packed, full, next_coeffs, peer):
    peer[...] = filled[...]
    for i in range(KEEP):
        peer[listed[i]] = arrived[i]
    mix(kept, peer, own, kept_coeffs, packed, full, next_coeffs)


def base_kernel(kept, peer, coeffs, kept_coeffs, next_coeffs, moved, weight, out, left_high, right_high, delta):
    delta[...] = step * peer[...].astype(f32) - 2 * step * coeffs[...]
    for i in range(KEEP):
        s = kept[i]
        delta[s] = step * (peer[s].astype(f32) - kept_coeffs[i] - next_coeffs[i])
    grid = from_slabs(lambda s: delta[s]) + moved[...]
    left, right = split(left_table_t()), split(right_table_t())
    left_high[...] = left[0]
    right_high[...] = right[0]
    out[...] = weight[...].astype(f32) + left_dot(left, right_dot(grid, right))


def finish(get, base, left_t, right_t, out):
    grid = (step * from_slabs(lambda s: get(s).astype(f32))).astype(bf16)
    turned = dot(grid, right_t[...]).astype(bf16)
    out[...] = (base[...] + dot(left_t[...], turned)).astype(bf16)


def near_last_kernel(peer, base, left_t, right_t, out):
    finish(lambda s: peer[s], base, left_t, right_t, out)


def far_last_kernel(listed, arrived, filled, base, left_t, right_t, out, slabs):
    slabs[...] = filled[...]
    for i in range(KEEP):
        slabs[listed[i]] = arrived[i]
    finish(lambda s: slabs[s], base, left_t, right_t, out)


def call(kernel, outs, specs, scratch=(), flops=0, moves=0):
    return pl.pallas_call(
        kernel,
        out_shape=[jax.ShapeDtypeStruct(shape, kind) for shape, kind in outs],
        in_specs=specs,
        out_specs=[VM] * len(outs),
        scratch_shapes=list(scratch),
        compiler_params=pltpu.CompilerParams(vmem_limit_bytes=16 * 2**20),
        cost_estimate=pl.CostEstimate(flops=flops, bytes_accessed=moves, transcendentals=0),
    )


SLAB32 = ((SLABS, 16, 128), f32)
SLAB16 = ((SLABS, 16, 128), bf16)
KEPT32 = ((KEEP, 16, 128), f32)
KEPT16 = ((KEEP, 16, 128), bf16)
GRID32 = ((ROWS, COLS), f32)
GRID16 = ((ROWS, COLS), bf16)
REST = pltpu.SMEM((SLABS + 1,), i32)
ROOM32, ROOM16 = pltpu.VMEM((SLABS, 16, 128), f32), pltpu.VMEM((SLABS, 16, 128), bf16)


TWO_LEFT, TWO_RIGHT = ((2, ROWS, ROWS), bf16), ((2, COLS, COLS), bf16)


def do_public(kept, public):
    outs = [SLAB32, SLAB16, ((LEFT + 1, 16, 128), bf16), TWO_LEFT, TWO_RIGHT]
    return call(public_kernel, outs, [SM, VM], [REST], 10**9, 2**21)(kept, public)


def do_spread(count, own, other):
    return call(spread_kernel, [((count, 2) + own.shape, bf16)], [VM, VM], (), 10**5, 2**20)(own, other)[0]


def do_grads(count, place, way, grads, weight, right):
    outs = [(grads.shape, bf16), GRID16]
    return call(grads_kernel, outs, [SM] * 3 + [VM] * 3, (), 2 * 10**9, 2**22)(count, place, way, grads, weight, right)


def do_weights(kept, *rest):
    outs = [KEPT16, SLAB16, KEPT32, GRID32]
    return call(weights_kernel, outs, [SM] + [VM] * 5, [ROOM32], 3 * 10**8, 2**21)(kept, *rest)


def do_fill(listed, early):
    return call(fill_kernel, [SLAB16], [SM, VM], (), 10**6, 2**18)(listed, early)[0]


def do_near(kept, peer, own, kept_coeffs):
    return [*call(near_kernel, [KEPT16, SLAB16, KEPT32], [SM] + [VM] * 3, (), 10**6, 2**19)(kept, peer, own, kept_coeffs), peer]


def do_far(kept, listed, *rest):
    return list(call(far_kernel, [KEPT16, SLAB16, KEPT32, SLAB16], [SM, SM] + [VM] * 4, (), 10**6, 2**19)(kept, listed, *rest))


def do_base(kept, *rest):
    outs = [GRID32, ((ROWS, ROWS), bf16), ((COLS, COLS), bf16)]
    return call(base_kernel, outs, [SM] + [VM] * 6, [ROOM32], 10**9, 2**22)(kept, *rest)


def do_near_last(*args):
    return call(near_last_kernel, [GRID16], [VM] * 4, (), 2 * 10**8, 2**20)(*args)[0]


def do_far_last(listed, *rest):
    return call(far_last_kernel, [GRID16], [SM] + [VM] * 5, [ROOM16], 2 * 10**8, 2**20)(listed, *rest)[0]


def swapped(block, axis, bit):
    count = lax.axis_size(axis)
    return lax.ppermute(block, axis, [(i, i ^ (1 << bit)) for i in range(count)])


def peers_list(early):
    return early[LEFT, 0, :SLABS].astype(i32)


def shards(activations, out_grads, weight, public, counts, kept, distances):
    top = lax.axis_size("rep").bit_length() - 2
    count_x = lax.axis_size("tp") // 2
    groups = [[2 * x + z for x in range(count_x)] for z in range(2)]
    place = (lax.axis_index("tp") & 1).astype(i32)[None]
    acts, grads, weight, public, kept = activations[0], out_grads[0], weight[0], public[0], kept[0, 0]

    bits = lax.population_count(distances - 1)
    way = jnp.sum(jnp.where(bits == top, jnp.array([top, 0], i32), bits))
    ways = [(bit, top) for bit in range(top)] + [(top, bit) for bit in range(top)]
    known = lax.clamp(jnp.int32(0), way, jnp.int32(len(ways) - 1))[None]
    other = swapped(acts, "tp", 0)
    coeffs, public_full, early, left_two, right_two = do_public(kept, public)
    early_far = swapped(early, "rep", top)
    other, public_full = lax.optimization_barrier((other, public_full))
    pairs = do_spread(count_x, acts, other)
    pairs, counts = lax.optimization_barrier((pairs, counts))
    rows = lax.all_to_all(pairs, "tp", 0, 0, axis_index_groups=groups)
    turned, weight_turned = do_grads(counts, place, known, grads, weight, right_two)
    packed, full, kept_coeffs, moved = do_weights(kept, rows, turned, weight_turned, left_two, public_full)

    def rounds(first, second):
        def run(packed, full, early_far):
            listed = peers_list(early_far)
            filled = do_fill(listed, early_far)
            if first == top:
                packed, full, next_coeffs, peer = do_far(kept, listed, swapped(packed, "rep", first), filled, full, kept_coeffs)
            else:
                packed, full, next_coeffs, peer = do_near(kept, swapped(full, "rep", first), full, kept_coeffs)
            arrived = swapped(packed if second == top else full, "rep", second)
            last = do_base(kept, peer, coeffs, kept_coeffs, next_coeffs, moved, weight)
            if second == top:
                return do_far_last(listed, arrived, filled, *last)
            return do_near_last(arrived, *last)

        return run

    return lax.switch(way, [rounds(*pair) for pair in ways], packed, full, early_far)[None]


def solution(mesh):
    return jax.shard_map(
        shards,
        mesh=mesh,
        in_specs=(
            P("rep", "tp", None),
            P("rep", None, "tp"),
            P("rep", None, "tp"),
            P("rep", None, "tp"),
            P("rep"),
            P("rep", "tp", None),
            P(),
        ),
        out_specs=P("rep", None, "tp"),
        check_vma=False,
    )
```

time: 60.2 us -> 67.9 us (1.13)
  the two profiles are of different devices: /device:TPU:1 before, /device:TPU:19 now
where the time goes in v3:
time: 67.9 us; the launch traced here: 67.5 us
  starting transfers between devices  26.7 us (39%)
  waiting for transfers between devices  18.6 us (27%)
  Pallas kernels  13.6 us (20%)
  local copies, waits for them, and re-layouts  5.21 us (8%)
  between operations  1.45 us (2%)
  other arithmetic  1.27 us (2%)
    ppermute x4, starting transfers between devices, swapped(): return lax.ppermute(block, axis, [(i, i ^ 1 << bit) for i in range(count)])  22.4 us
    ppermute x4, waiting for transfers between devices, swapped(): return lax.ppermute(block, axis, [(i, i ^ 1 << bit) for i in range(count)])  18.6 us
    unnamed x22, local copies, waits for them, and re-layouts  5.21 us
    all_to_all x1, starting transfers between devices, shards(): rows = lax.all_to_all(pairs, 'tp', 0, 0, axis_index_groups=groups)  4.27 us
    pallas_call x1, Pallas kernels, do_public(): call(public_kernel, outs, [SM, VM], [REST], 10 ** 9, 2 ** 21)(kept, public)  3.43 us
    pallas_call x1, Pallas kernels, do_base(): call(base_kernel, outs, [SM] + [VM] * 6, [ROOM32], 10 ** 9, 2 ** 22)  3.02 us
    pallas_call x1, Pallas kernels, do_grads(): call(grads_kernel, outs, [SM] * 3 + [VM] * 3, (), 2 * 10 ** 9, 2 ** 22)  1.92 us
    pallas_call x1, Pallas kernels, do_weights(): call(weights_kernel, outs, [SM] + [VM] * 5, [ROOM32], 3 * 10 ** 8, 2 ** 21)  1.6 us
  transfers between devices with their start and end apart: 5, of which 2 were waited for; matrix products, arithmetic and copies ran while one was open for 2% of the time, Pallas kernels for 16%

profile of v3, /device:TPU:19, one launch (start us, length us, event | category | flops | bytes accessed | tf_op | source)
XLA Modules:
  0.0 67.5 jit_solution(4944379624582790204)
XLA Ops:
  0.0 10.6 %collective-permute-start.21 = (bf16[128,256]{1,0:T(8,128)(2,1)}, bf16[128,256]{1,0:T(8,128)(2,1)S(1)}, u32[]{:S(2)}, u32[]{:S(2)}) collective-permute-start(bf16[128,256]{1,0:T(8,128)(2,1)} %bitcast.47), channel_id=1, source_target_pairs={{0,1},{1,0},{2,3},{3,2},{4,5},{5,4},{6,7},{7,6},{8,9},{9,8},{10,11... | collective-permute-start | bytes 196616 | tf_op jit(solution)/shard_map/ppermute | solution.py:329
  10.6 0.6 copy-done.6
  11.3 0.9 %copy-done.2 = bf16[1,256,512]{2,1,0:T(8,128)(2,1)S(1)} copy-done((bf16[1,256,512]{2,1,0:T(8,128)(2,1)S(1)}, bf16[1,256,512]{2,1,0:T(8,128)(2,1)}, u32[]{:S(2)}) %copy-start.2) | copy-done | bytes 262168
  12.2 3.4 %shard_map.92 = (f32[64,16,128]{2,1,0:T(8,128)}, bf16[64,16,128]{2,1,0:T(8,128)(2,1)S(1)}, bf16[25,16,128]{2,1,0:T(8,128)(2,1)S(1)}, bf16[2,256,256]{2,1,0:T(8,128)(2,1)S(1)}, bf16[2,512,512]{2,1,0:T(8,128)(2,1)S(1)}) custom-call(s32[40]{0:T(128)S(1)} %bitcast.61, bf16[256,512]{1,0:T(8,128)(2,1)S(1)} %bitcast.50), custom_call_target="tpu_custom_call" | custom-call | flops 1000000000 | bytes 2097152 | tf_op jit(solution)/shard_map/pallas_call | solution.py:285
  15.7 1.0 %copy-done.3 = bf16[2,512,512]{2,1,0:T(8,128)(2,1)} copy-done((bf16[2,512,512]{2,1,0:T(8,128)(2,1)}, bf16[2,512,512]{2,1,0:T(8,128)(2,1)S(1)}, u32[]{:S(2)}) %copy-start.3) | copy-done | bytes 1048600
  16.7 0.0 collective-permute-done.21.other
  16.7 0.8 %shard_map.93 = bf16[4,2,128,256]{3,2,1,0:T(8,128)(2,1)} custom-call(bf16[128,256]{1,0:T(8,128)(2,1)S(1)} %bitcast.48, bf16[128,256]{1,0:T(8,128)(2,1)S(1)} %collective-permute-done.21.other), custom_call_target="tpu_custom_call" | custom-call | flops 100000 | bytes 1048576 | tf_op jit(solution)/shard_map/pallas_call | solution.py:289
  17.5 4.3 %all-to-all-start = ((bf16[4,2,128,256]{3,2,1,0:T(8,128)(2,1)}), bf16[4,2,128,256]{3,2,1,0:T(8,128)(2,1)S(1)}, u32[]{:S(2)}, u32[]{:S(2)}) async-start(bf16[4,2,128,256]{3,2,1,0:T(8,128)(2,1)} %shard_map.93), calls=%async_computation | async-start | bytes 1048576 | tf_op jit(solution)/shard_map/all_to_all | solution.py:353
  21.8 4.0 %collective-permute-start.20 = (bf16[25,16,128]{2,1,0:T(8,128)(2,1)S(1)}, bf16[25,16,128]{2,1,0:T(8,128)(2,1)}, u32[]{:S(2)}, u32[]{:S(2)}) collective-permute-start(bf16[25,16,128]{2,1,0:T(8,128)(2,1)S(1)} %get-tuple-element.312), channel_id=1, source_target_pairs={{0,256},{8,264},{16,272},{24,280},{32,288},{40,296},{48,304},{56,3... | collective-permute-start | bytes 307208 | tf_op jit(solution)/shard_map/ppermute | solution.py:329
  26.5 0.0 copy-start.8
  26.5 0.0 copy-start.9
  26.5 0.6 copy-done.8
  27.1 0.0 copy-done.9
  27.1 0.6 fusion
  28.4 1.2 %copy-done.4 = bf16[2,512,512]{2,1,0:T(8,128)(2,1)S(1)} copy-done((bf16[2,512,512]{2,1,0:T(8,128)(2,1)S(1)}, bf16[2,512,512]{2,1,0:T(8,128)(2,1)}, u32[]{:S(2)}) %copy-start.4) | copy-done | bytes 1048600
  29.7 1.9 %shard_map.94 = (bf16[1024,512]{1,0:T(8,128)(2,1)S(1)}, bf16[256,512]{1,0:T(8,128)(2,1)S(1)}) custom-call(s32[1]{0:T(128)S(6)} %copy.29.count, s32[1]{0:T(128)} %bitcast.33.place, s32[1]{0:T(128)} %bitcast.34.way, bf16[1024,512]{1,0:T(8,128)(2,1)S(1)} %bitcast.49, bf16[256,512]{1,0:T(8,128)(2,1)} %bitcast.73, bf16[2,512,512]{2,1,0:T(8,128)(2,1)S(1)} %copy-done.4), custom_call_target="tpu_custom_call" | custom-call | flops 2000000000 | bytes 4194304 | tf_op jit(solution)/shard_map/pallas_call | solution.py:294
  31.6 0.0 all-to-all-done.acts
  31.6 0.0 copy-start.7
  31.6 1.6 %shard_map.95 = (bf16[40,16,128]{2,1,0:T(8,128)(2,1)S(1)}, bf16[64,16,128]{2,1,0:T(8,128)(2,1)S(1)}, f32[40,16,128]{2,1,0:T(8,128)S(1)}, f32[256,512]{1,0:T(8,128)S(1)}) custom-call(s32[40]{0:T(128)S(1)} %bitcast.62, bf16[4,2,128,256]{3,2,1,0:T(8,128)(2,1)S(1)} %all-to-all-done.acts, bf16[1024,512]{1,0:T(8,128)(2,1)S(1)} %get-tuple-element.318.turned, ...), custom_call_target="tpu_custom_call" | custom-call | flops 300000000 | bytes 2097152 | tf_op jit(solution)/shard_map/pallas_call | solution.py:299
  33.2 0.0 collective-permute-done.20
  33.3 33.5 %conditional.1 = (bf16[1,256,512]{2,1,0:T(8,128)(2,1)S(1)}) conditional(s32[]{:T(128)} %clamp.4, (bf16[25,16,128]{2,1,0:T(8,128)(2,1)}, bf16[64,16,128]{2,1,0:T(8,128)(2,1)S(1)}, s32[40]{0:T(128)S(1)}, f32[40,16,128]{2,1,0:T(8,128)S(1)}, f32[64,16,128]{2,1,0:T(8,128)S(1)}, /*index=5*/f32[256,512]{1,0:T(8,128)S(1)}, ...), branch_computations={%region_1.2_spmd, %region_2.3_spmd, %region_3.4_spmd, %region_4.5_... | conditional | flops 1202000128 | bytes 7733720 | solution.py:373
  33.5 2.2 %collective-permute-start.16 = (bf16[40,16,128]{2,1,0:T(8,128)(2,1)S(1)}, bf16[40,16,128]{2,1,0:T(8,128)(2,1)S(1)}, u32[]{:S(2)}, u32[]{:S(2)}) collective-permute-start(bf16[40,16,128]{2,1,0:T(8,128)(2,1)S(1)} %get-tuple-element.271), channel_id=1, source_target_pairs={{0,256},{8,264},{16,272},{24,280},{32,288},{40,296},{48,304},{56,3... | collective-permute-start | bytes 491528 | tf_op jit(solution)/shard_map/cond/branch_8_fun/ppermute | solution.py:329
  35.7 0.6 bitcast_convert_fusion.8.listed
  36.4 1.0 %branch_8_fun.4.filled = bf16[64,16,128]{2,1,0:T(8,128)(2,1)S(1)} custom-call(s32[64]{0:T(128)S(1)} %bitcast_convert_fusion.8.listed, bf16[25,16,128]{2,1,0:T(8,128)(2,1)} %get-tuple-element.270.early), custom_call_target="tpu_custom_call" | custom-call | flops 1000000 | bytes 262144 | tf_op jit(solution)/shard_map/cond/branch_8_fun/pallas_call | solution.py:303
  37.3 7.7 %collective-permute-done.16.arrived = bf16[40,16,128]{2,1,0:T(8,128)(2,1)S(1)} collective-permute-done((bf16[40,16,128]{2,1,0:T(8,128)(2,1)S(1)}, bf16[40,16,128]{2,1,0:T(8,128)(2,1)S(1)}, u32[]{:S(2)}, u32[]{:S(2)}) %collective-permute-start.16) | collective-permute-done | bytes 163872 | tf_op jit(solution)/shard_map/cond/branch_8_fun/ppermute | solution.py:329
  45.0 1.3 %branch_8_fun.5 = (bf16[40,16,128]{2,1,0:T(8,128)(2,1)}, bf16[64,16,128]{2,1,0:T(8,128)(2,1)S(1)}, f32[40,16,128]{2,1,0:T(8,128)S(1)}, bf16[64,16,128]{2,1,0:T(8,128)(2,1)S(1)}) custom-call(s32[40]{0:T(128)S(1)} %get-tuple-element.269.kept, s32[64]{0:T(128)S(1)} %bitcast_convert_fusion.8.listed, bf16[40,16,128]{2,1,0:T(8,128)(2,1)S(1)} %collective-permute-done.16.arrived, ...), custom_call_target="tpu_custom_call" | custom-call | flops 1000000 | bytes 524288 | tf_op jit(solution)/shard_map/cond/branch_8_fun/pallas_call | solution.py:311
  46.3 5.6 %collective-permute-start.17 = (bf16[64,16,128]{2,1,0:T(8,128)(2,1)S(1)}, bf16[64,16,128]{2,1,0:T(8,128)(2,1)S(1)}, u32[]{:S(2)}, u32[]{:S(2)}) collective-permute-start(bf16[64,16,128]{2,1,0:T(8,128)(2,1)S(1)} %get-tuple-element.274), channel_id=1, source_target_pairs={{0,64},{8,72},{16,80},{24,88},{32,96},{40,104},{48,112},{56,120},{... | collective-permute-start | bytes 786440 | tf_op jit(solution)/shard_map/cond/branch_8_fun/ppermute | solution.py:329
  52.0 3.0 %branch_8_fun.6 = (f32[256,512]{1,0:T(8,128)S(1)}, bf16[256,256]{1,0:T(8,128)(2,1)S(1)}, bf16[512,512]{1,0:T(8,128)(2,1)S(1)}) custom-call(s32[40]{0:T(128)S(1)} %get-tuple-element.269.kept, bf16[64,16,128]{2,1,0:T(8,128)(2,1)S(1)} %get-tuple-element.275.peer, f32[64,16,128]{2,1,0:T(8,128)S(1)} %get-tuple-element.276.coeffs, ...), custom_call_target="tpu_custom_call" | custom-call | flops 1000000000 | bytes 4194304 | tf_op jit(solution)/shard_map/cond/branch_8_fun/pallas_call | solution.py:316
  55.0 10.9 %collective-permute-done.17.peer = bf16[64,16,128]{2,1,0:T(8,128)(2,1)S(1)} collective-permute-done((bf16[64,16,128]{2,1,0:T(8,128)(2,1)S(1)}, bf16[64,16,128]{2,1,0:T(8,128)(2,1)S(1)}, u32[]{:S(2)}, u32[]{:S(2)}) %collective-permute-start.17) | collective-permute-done | bytes 262176 | tf_op jit(solution)/shard_map/cond/branch_8_fun/ppermute | solution.py:329
  65.9 0.5 branch_8_fun.7
  66.7 0.0 copy-start.5
  66.8 0.7 %copy-done.5 = bf16[1,256,512]{2,1,0:T(8,128)(2,1)} copy-done((bf16[1,256,512]{2,1,0:T(8,128)(2,1)}, bf16[1,256,512]{2,1,0:T(8,128)(2,1)S(1)}, u32[]{:S(2)}) %copy-start.5) | copy-done | bytes 262168
  (11 shorter events, 0.0 us)
Async XLA Ops:
  0.0 16.7 %collective-permute-start.21 = (bf16[128,256]{1,0:T(8,128)(2,1)}, bf16[128,256]{1,0:T(8,128)(2,1)S(1)}, u32[]{:S(2)}, u32[]{:S(2)}) collective-permute-start(bf16[128,256]{1,0:T(8,128)(2,1)} %bitcast.47), channel_id=1, source_target_pairs={{0,1},{1,0},{2,3},{3,2},{4,5},{5,4},{6,7},{7,6},{8,9},{9,8},{10,11... | collective-permute-start | bytes 196616 | tf_op jit(solution)/shard_map/ppermute | solution.py:329
  10.6 0.7 copy-start.6
  11.3 0.9 %copy-start.2 = (bf16[1,256,512]{2,1,0:T(8,128)(2,1)S(1)}, bf16[1,256,512]{2,1,0:T(8,128)(2,1)}, u32[]{:S(2)}) copy-start(bf16[1,256,512]{2,1,0:T(8,128)(2,1)} %param.21) | copy-start | bytes 786436
  12.2 4.5 %copy-start = (bf16[1,128,256]{2,1,0:T(8,128)(2,1)S(1)}, bf16[1,128,256]{2,1,0:T(8,128)(2,1)}, u32[]{:S(2)}) copy-start(bf16[1,128,256]{2,1,0:T(8,128)(2,1)} %param.18) | copy-start | bytes 196612
  15.7 1.0 %copy-start.3 = (bf16[2,512,512]{2,1,0:T(8,128)(2,1)}, bf16[2,512,512]{2,1,0:T(8,128)(2,1)S(1)}, u32[]{:S(2)}) copy-start(bf16[2,512,512]{2,1,0:T(8,128)(2,1)S(1)} %get-tuple-element.317.right) | copy-start | bytes 3145732
  16.7 11.7 %copy-start.1 = (bf16[1,1024,512]{2,1,0:T(8,128)(2,1)S(1)}, bf16[1,1024,512]{2,1,0:T(8,128)(2,1)}, u32[]{:S(2)}) copy-start(bf16[1,1024,512]{2,1,0:T(8,128)(2,1)} %param.19) | copy-start | bytes 3145732
  17.5 14.1 %all-to-all-start = ((bf16[4,2,128,256]{3,2,1,0:T(8,128)(2,1)}), bf16[4,2,128,256]{3,2,1,0:T(8,128)(2,1)S(1)}, u32[]{:S(2)}, u32[]{:S(2)}) async-start(bf16[4,2,128,256]{3,2,1,0:T(8,128)(2,1)} %shard_map.93), calls=%async_computation | async-start | bytes 1048576 | tf_op jit(solution)/shard_map/all_to_all | solution.py:353
  21.8 11.4 %collective-permute-start.20 = (bf16[25,16,128]{2,1,0:T(8,128)(2,1)S(1)}, bf16[25,16,128]{2,1,0:T(8,128)(2,1)}, u32[]{:S(2)}, u32[]{:S(2)}) collective-permute-start(bf16[25,16,128]{2,1,0:T(8,128)(2,1)S(1)} %get-tuple-element.312), channel_id=1, source_target_pairs={{0,256},{8,264},{16,272},{24,280},{32,288},{40,296},{48,304},{56,3... | collective-permute-start | bytes 307208 | tf_op jit(solution)/shard_map/ppermute | solution.py:329
  26.5 0.7 copy-start.8
  26.5 0.7 copy-start.9
  28.4 1.2 %copy-start.4 = (bf16[2,512,512]{2,1,0:T(8,128)(2,1)S(1)}, bf16[2,512,512]{2,1,0:T(8,128)(2,1)}, u32[]{:S(2)}) copy-start(bf16[2,512,512]{2,1,0:T(8,128)(2,1)} %copy-done.3) | copy-start | bytes 3145732
  31.6 1.6 %copy-start.7 = (bf16[1,256,512]{2,1,0:T(8,128)(2,1)S(1)}, bf16[1,256,512]{2,1,0:T(8,128)(2,1)}, u32[]{:S(2)}) copy-start(bf16[1,256,512]{2,1,0:T(8,128)(2,1)} %param.20) | copy-start | bytes 786436
  31.6 1.6 %copy-start.10 = (f32[64,16,128]{2,1,0:T(8,128)S(1)}, f32[64,16,128]{2,1,0:T(8,128)}, u32[]{:S(2)}) copy-start(f32[64,16,128]{2,1,0:T(8,128)} %get-tuple-element.324) | copy-start | bytes 1572868
  33.5 11.5 %collective-permute-start.16 = (bf16[40,16,128]{2,1,0:T(8,128)(2,1)S(1)}, bf16[40,16,128]{2,1,0:T(8,128)(2,1)S(1)}, u32[]{:S(2)}, u32[]{:S(2)}) collective-permute-start(bf16[40,16,128]{2,1,0:T(8,128)(2,1)S(1)} %get-tuple-element.271), channel_id=1, source_target_pairs={{0,256},{8,264},{16,272},{24,280},{32,288},{40,296},{48,304},{56,3... | collective-permute-start | bytes 491528 | tf_op jit(solution)/shard_map/cond/branch_8_fun/ppermute | solution.py:329
  46.3 19.6 %collective-permute-start.17 = (bf16[64,16,128]{2,1,0:T(8,128)(2,1)S(1)}, bf16[64,16,128]{2,1,0:T(8,128)(2,1)S(1)}, u32[]{:S(2)}, u32[]{:S(2)}) collective-permute-start(bf16[64,16,128]{2,1,0:T(8,128)(2,1)S(1)} %get-tuple-element.274), channel_id=1, source_target_pairs={{0,64},{8,72},{16,80},{24,88},{32,96},{40,104},{48,112},{56,120},{... | collective-permute-start | bytes 786440 | tf_op jit(solution)/shard_map/cond/branch_8_fun/ppermute | solution.py:329
  66.7 0.7 %copy-start.5 = (bf16[1,256,512]{2,1,0:T(8,128)(2,1)}, bf16[1,256,512]{2,1,0:T(8,128)(2,1)S(1)}, u32[]{:S(2)}) copy-start(bf16[1,256,512]{2,1,0:T(8,128)(2,1)S(1)} %get-tuple-element.377) | copy-start | bytes 786436

commit v4 on v3

v4 whole, which is shorter than its diff:
```python
import jax
import jax.numpy as jnp
import numpy as np
from jax import lax
from jax.experimental import pallas as pl
from jax.experimental.pallas import tpu as pltpu
from jax.sharding import PartitionSpec as P


learn_rate = 0.02
step = 0.25
ROWS, COLS, KEEP, SLABS, TOP = 256, 512, 40, 64, 5
LEFT = SLABS - KEEP
f32, bf16, i32 = jnp.float32, jnp.bfloat16, jnp.int32
VM = pl.BlockSpec(memory_space=pltpu.VMEM)
SM = pl.BlockSpec(memory_space=pltpu.SMEM)


def cosines(freq, place):
    phase = ((2 * place + 1) * freq) & 255
    scale = jnp.where(freq == 0, np.float32(np.sqrt(1 / 64)), np.float32(np.sqrt(2 / 64)))
    return scale * jnp.cos(phase.astype(f32) * np.float32(np.pi / 128))


def lines(shape, axis):
    return lax.broadcasted_iota(i32, shape, axis)


def spectrum():
    shape = (64, 128)
    return cosines(lines(shape, 0), lines(shape, 1) & 63)


def left_table(table):
    groups = [table[8 * ub : 8 * ub + 8] for ub in range(8) for _ in range(2)]
    shape = (128, 128)
    return jnp.where((lines(shape, 0) >> 3) & 1 == lines(shape, 1) >> 6, jnp.concatenate(groups, 0), 0.0)


def left_table_t():
    shape = (64, 128)
    r = lines(shape, 1)
    part = cosines((r >> 4) * 8 + (r & 7), lines(shape, 0))
    odd = (r >> 3) & 1
    return jnp.concatenate([jnp.where(odd == 0, part, 0.0), jnp.where(odd == 1, part, 0.0)], 0)


def right_table():
    shape = (64, COLS)
    j = lines(shape, 1)
    part = cosines((j >> 6) * 8 + (j & 7), lines(shape, 0))
    tile = (j >> 3) & 7
    return jnp.concatenate([jnp.where(tile == b, part, 0.0).astype(bf16) for b in range(8)], 0)


def right_table_t():
    table = spectrum()
    low = lines(table.shape, 1) < 64
    masked = jnp.where(low, table, 0.0), jnp.where(low, 0.0, table)
    zeros = jnp.zeros((8, 128), f32)
    columns = []
    for c in range(4):
        groups = [masked[b & 1][8 * vb : 8 * vb + 8] if b >> 1 == c else zeros for vb in range(8) for b in range(8)]
        columns.append(jnp.concatenate(groups, 0))
    return jnp.concatenate(columns, 1)


def dot(a, b):
    return jnp.dot(a, b, preferred_element_type=f32)


def split(x):
    high = x.astype(bf16)
    return high, (x - high.astype(f32)).astype(bf16)


def by_halves(run, x):
    return jnp.concatenate([run(x[:128]), run(x[128:])], 0)


def left_dot(table, x):
    high, low = split(x)
    return dot(table[0], high) + (dot(table[0], low) + dot(table[1], high))


def right_dot(x, table):
    high, low = split(x)
    return dot(high, table[0]) + (dot(low, table[0]) + dot(high, table[1]))


def low_lanes():
    return lax.broadcasted_iota(i32, (128, 128), 1) < 64


def to_slabs(grid, put):
    low = low_lanes()
    for q in range(4):
        top = grid[:128, 128 * q : 128 * (q + 1)]
        bottom = grid[128:, 128 * q : 128 * (q + 1)]
        even = jnp.where(low, top, pltpu.roll(bottom, 64, 1))
        odd = jnp.where(low, pltpu.roll(top, 64, 1), bottom)
        for ub in range(8):
            put(ub * 8 + 2 * q, even[16 * ub : 16 * (ub + 1)])
            put(ub * 8 + 2 * q + 1, odd[16 * ub : 16 * (ub + 1)])


def from_slabs(get):
    low = low_lanes()
    tops, bottoms = [], []
    for q in range(4):
        even = jnp.concatenate([get(ub * 8 + 2 * q) for ub in range(8)], 0)
        odd = jnp.concatenate([get(ub * 8 + 2 * q + 1) for ub in range(8)], 0)
        tops.append(jnp.where(low, even, pltpu.roll(odd, 64, 1)))
        bottoms.append(jnp.where(low, pltpu.roll(even, 64, 1), odd))
    return jnp.concatenate([jnp.concatenate(tops, 1), jnp.concatenate(bottoms, 1)], 0)


def list_all(kept, room):
    room[...] = jnp.full((1, 128), -1, i32)
    room[:, :KEEP] = kept[...]
    named = room[...]
    shape = (SLABS, 128)
    s, lane = lines(shape, 0), lines(shape, 1)
    hits = jnp.where(s == named, 1.0, 0.0)
    free = jnp.broadcast_to(1.0 - jnp.max(hits, axis=1, keepdims=True), shape)
    shape = (SLABS, SLABS)
    below = jnp.where(lines(shape, 1) < lines(shape, 0), 1.0, 0.0)
    rank = dot(below.astype(bf16), free.astype(bf16))
    here = jnp.where((lane - KEEP).astype(f32) == rank, free, 0.0)
    rest = jnp.sum(here * s.astype(f32), axis=0, keepdims=True)
    row = jnp.where(lane[:1] < KEEP, named.astype(f32), rest)
    room[...] = row.astype(i32)
    return row


def find_way(distances, way):
    sizes = [sum((distances[k] > 1 << bit).astype(i32) for bit in range(TOP)) for k in range(2)]
    way[0] = jnp.where(sizes[1] == TOP, sizes[0], TOP + sizes[1])


def public_kernel(distances, kept, public, acts, coeffs, full, early, pairs, way, room, listed, sems, sem):
    count_x = pairs.shape[0]
    copies = [pltpu.make_async_copy(acts, pairs.at[x, 0], sems.at[x]) for x in range(count_x)]
    for copy in copies:
        copy.start()
    find_way(distances, way)
    row = list_all(kept, room)
    to_scalars = pltpu.make_async_copy(room, listed, sem.at[0])
    to_scalars.start()
    left, right = left_table(spectrum()).astype(bf16), right_table()
    grid = by_halves(lambda x: dot(left, x), dot(public[...], right).astype(bf16))

    def put(s, slab):
        coeffs[s] = slab
        full[s] = slab.astype(bf16)

    to_slabs(grid, put)
    early[LEFT] = jnp.broadcast_to(row, (16, 128)).astype(bf16)
    to_scalars.wait()
    for j in range(LEFT):
        early[j] = full[listed[0, KEEP + j]]
    for copy in copies:
        copy.wait()


def spread_kernel(other, pairs, out, sems):
    copies = [pltpu.make_async_copy(other, out.at[x, 1], sems.at[x]) for x in range(out.shape[0])]
    for copy in copies:
        copy.start()
    for copy in copies:
        copy.wait()


def own_place():
    return lax.axis_index("tp") & 1


def grads_kernel(count, grads, weight, turned, weight_turned):
    place = own_place()
    right = right_table()
    part = grads.shape[0] // 4
    for k in range(4):
        y = dot(grads[k * part : (k + 1) * part], right)
        token = k * part + lines((part, COLS), 0)
        y = jnp.where(token < count[...], y, 0.0).astype(bf16)
        for z in range(2):
            to = k * part + ((z + place) & 1) * (part // 2)
            turned[pl.ds(pl.multiple_of(to, part // 2), part // 2), :] = y[part // 2 * z : part // 2 * (z + 1)]
    weight_turned[...] = dot(weight[...], right).astype(bf16)


def weights_kernel(kept, acts, turned, weight_turned, public_full, packed, full, kept_coeffs, moved, slabs):
    left = split(left_table(spectrum()))
    dims = (((1,), (1,)), ((), ()))
    x = acts[...].reshape(-1, ROWS)
    rows = []
    for h in range(2):
        half = x[:, 128 * h : 128 * (h + 1)]
        row = lax.dot_general(left[0], half, dims, preferred_element_type=f32)
        rows.append((row + lax.dot_general(left[1], half, dims, preferred_element_type=f32)).astype(bf16))
    change = -learn_rate * dot(jnp.concatenate(rows, 0), turned[...])
    moved[...] = change

    def put(s, slab):
        slabs[s] = slab

    to_slabs(by_halves(lambda x: dot(left[0], x), weight_turned[...]) + change, put)
    full[...] = public_full[...]
    for i in range(KEEP):
        s = kept[i]
        slab = slabs[s]
        short = slab.astype(bf16)
        kept_coeffs[i] = slab
        packed[i] = short
        full[s] = short


def fill_kernel(listed, early, peer):
    for j in range(LEFT):
        peer[listed[KEEP + j]] = early[j]
    for i in range(KEEP):
        peer[listed[i]] = jnp.zeros((16, 128), bf16)


def mix(kept, peer, own, kept_coeffs, packed, full, next_coeffs):
    full[...] = own[...]
    for i in range(KEEP):
        s = kept[i]
        value = kept_coeffs[i]
        value = value + step * (peer[s].astype(f32) - value)
        short = value.astype(bf16)
        next_coeffs[i] = value
        packed[i] = short
        full[s] = short


def near_kernel(kept, peer, own, kept_coeffs, packed, full, next_coeffs):
    mix(kept, peer, own, kept_coeffs, packed, full, next_coeffs)


def far_kernel(kept, listed, arrived, filled, own, kept_coeffs, packed, full, next_coeffs, peer):
    peer[...] = filled[...]
    for i in range(KEEP):
        peer[listed[i]] = arrived[i]
    mix(kept, peer, own, kept_coeffs, packed, full, next_coeffs)


def base_kernel(kept, peer, coeffs, kept_coeffs, next_coeffs, moved, weight, out, left_high, right_high, delta):
    delta[...] = step * peer[...].astype(f32) - 2 * step * coeffs[...]
    for i in range(KEEP):
        s = kept[i]
        delta[s] = step * (peer[s].astype(f32) - kept_coeffs[i] - next_coeffs[i])
    grid = from_slabs(lambda s: delta[s]) + moved[...]
    left, right = split(left_table_t()), split(right_table_t())
    left_high[...] = left[0]
    right_high[...] = right[0]
    out[...] = weight[...].astype(f32) + by_halves(lambda x: left_dot(left, x), right_dot(grid, right))


def finish(get, base, left_t, right_t, out):
    grid = (step * from_slabs(lambda s: get(s).astype(f32))).astype(bf16)
    turned = dot(grid, right_t[...]).astype(bf16)
    out[...] = (base[...] + by_halves(lambda x: dot(left_t[...], x), turned)).astype(bf16)


def near_last_kernel(peer, base, left_t, right_t, out):
    finish(lambda s: peer[s], base, left_t, right_t, out)


def far_last_kernel(listed, arrived, filled, base, left_t, right_t, out, slabs):
    slabs[...] = filled[...]
    for i in range(KEEP):
        slabs[listed[i]] = arrived[i]
    finish(lambda s: slabs[s], base, left_t, right_t, out)


def call(kernel, outs, specs, scratch=(), flops=0, moves=0, out_specs=None, aliases=None):
    return pl.pallas_call(
        kernel,
        out_shape=[jax.ShapeDtypeStruct(shape, kind) for shape, kind in outs],
        in_specs=specs,
        out_specs=out_specs or [VM] * len(outs),
        scratch_shapes=list(scratch),
        input_output_aliases=aliases or {},
        compiler_params=pltpu.CompilerParams(vmem_limit_bytes=16 * 2**20),
        cost_estimate=pl.CostEstimate(flops=flops, bytes_accessed=moves, transcendentals=0),
    )


SLAB32 = ((SLABS, 16, 128), f32)
SLAB16 = ((SLABS, 16, 128), bf16)
KEPT32 = ((KEEP, 16, 128), f32)
KEPT16 = ((KEEP, 16, 128), bf16)
GRID32 = ((ROWS, COLS), f32)
GRID16 = ((ROWS, COLS), bf16)
REST = pltpu.SMEM((SLABS + 1,), i32)
ROOM32, ROOM16 = pltpu.VMEM((SLABS, 16, 128), f32), pltpu.VMEM((SLABS, 16, 128), bf16)


ANY = pl.BlockSpec(memory_space=pl.ANY)


def sems(count):
    return pltpu.SemaphoreType.DMA((count,))


def do_public(count, distances, kept, public, acts):
    outs = [SLAB32, SLAB16, ((LEFT + 1, 16, 128), bf16), ((count, 2) + acts.shape, bf16), ((1,), i32)]
    scratch = [pltpu.VMEM((1, 128), i32), pltpu.SMEM((1, 128), i32), sems(count), sems(1)]
    return call(public_kernel, outs, [SM, VM, VM, ANY], scratch, 10**9, 2**21, [VM, VM, VM, ANY, SM])(distances, kept, public, acts)


def do_spread(other, pairs):
    outs = [(pairs.shape, bf16)]
    return call(spread_kernel, outs, [VM, ANY], [sems(pairs.shape[0])], 10**5, 2**20, [ANY], {1: 0})(other, pairs)[0]


def do_grads(count, grads, weight):
    return call(grads_kernel, [(grads.shape, bf16), GRID16], [VM] * 3, (), 2 * 10**9, 2**22)(count, grads, weight)


def do_weights(kept, *rest):
    outs = [KEPT16, SLAB16, KEPT32, GRID32]
    return call(weights_kernel, outs, [SM] + [VM] * 4, [ROOM32], 3 * 10**8, 2**21)(kept, *rest)


def do_fill(listed, early):
    return call(fill_kernel, [SLAB16], [SM, VM], (), 10**6, 2**18)(listed, early)[0]


def do_near(kept, peer, own, kept_coeffs):
    return [*call(near_kernel, [KEPT16, SLAB16, KEPT32], [SM] + [VM] * 3, (), 10**6, 2**19)(kept, peer, own, kept_coeffs), peer]


def do_far(kept, listed, *rest):
    return list(call(far_kernel, [KEPT16, SLAB16, KEPT32, SLAB16], [SM, SM] + [VM] * 4, (), 10**6, 2**19)(kept, listed, *rest))


def do_base(kept, *rest):
    outs = [GRID32, ((128, 128), bf16), ((COLS, COLS), bf16)]
    return call(base_kernel, outs, [SM] + [VM] * 6, [ROOM32], 10**9, 2**22)(kept, *rest)


def do_near_last(*args):
    return call(near_last_kernel, [GRID16], [VM] * 4, (), 2 * 10**8, 2**20)(*args)[0]


def do_far_last(listed, *rest):
    return call(far_last_kernel, [GRID16], [SM] + [VM] * 5, [ROOM16], 2 * 10**8, 2**20)(listed, *rest)[0]


def swapped(block, axis, bit):
    count = lax.axis_size(axis)
    return lax.ppermute(block, axis, [(i, i ^ (1 << bit)) for i in range(count)])


def peers_list(early):
    return early[LEFT, 0, :SLABS].astype(i32)


def shards(activations, out_grads, weight, public, counts, kept, distances):
    top = TOP
    count_x = lax.axis_size("tp") // 2
    groups = [[2 * x + z for x in range(count_x)] for z in range(2)]
    acts, grads, weight, public, kept = activations[0], out_grads[0], weight[0], public[0], kept[0, 0]

    other = swapped(acts, "tp", 0)
    coeffs, public_full, early, pairs, way = do_public(count_x, distances, kept[None], public, acts)
    early_far = swapped(early, "rep", top)
    pairs = do_spread(other, pairs)
    pairs, counts = lax.optimization_barrier((pairs, counts[:, None]))
    rows = lax.all_to_all(pairs, "tp", 0, 0, axis_index_groups=groups)
    turned, weight_turned = do_grads(counts, grads, weight)
    packed, full, kept_coeffs, moved = do_weights(kept, rows, turned, weight_turned, public_full)

    def rounds(first, second):
        def run(packed, full, early_far):
            listed = peers_list(early_far)
            filled = do_fill(listed, early_far)
            if first == top:
                packed, full, next_coeffs, peer = do_far(kept, listed, swapped(packed, "rep", first), filled, full, kept_coeffs)
            else:
                packed, full, next_coeffs, peer = do_near(kept, swapped(full, "rep", first), full, kept_coeffs)
            arrived = swapped(packed if second == top else full, "rep", second)
            last = do_base(kept, peer, coeffs, kept_coeffs, next_coeffs, moved, weight)
            if second == top:
                return do_far_last(listed, arrived, filled, *last)
            return do_near_last(arrived, *last)

        return run

    ways = [(bit, top) for bit in range(top)] + [(top, bit) for bit in range(top)]
    return lax.switch(way[0], [rounds(*pair) for pair in ways], packed, full, early_far)[None]


def solution(mesh):
    return jax.shard_map(
        shards,
        mesh=mesh,
        in_specs=(
            P("rep", "tp", None),
            P("rep", None, "tp"),
            P("rep", None, "tp"),
            P("rep", None, "tp"),
            P("rep"),
            P("rep", "tp", None),
            P(),
        ),
        out_specs=P("rep", None, "tp"),
        check_vma=False,
    )
```

time: 67.9 us -> 51.9 us (0.76)
  the two profiles are of different devices: /device:TPU:19 before, /device:TPU:1 now
where the time goes in v4:
time: 51.9 us; the launch traced here: 51.5 us
  starting transfers between devices  27.8 us (54%)
  Pallas kernels  12 us (23%)
  waiting for transfers between devices  6.81 us (13%)
  local copies, waits for them, and re-layouts  3.16 us (6%)
  between operations  1.43 us (3%)
    ppermute x4, starting transfers between devices, swapped(): return lax.ppermute(block, axis, [(i, i ^ 1 << bit) for i in range(count)])  23.8 us
    ppermute x4, waiting for transfers between devices, swapped(): return lax.ppermute(block, axis, [(i, i ^ 1 << bit) for i in range(count)])  6.42 us
    all_to_all x1, starting transfers between devices, shards(): rows = lax.all_to_all(pairs, 'tp', 0, 0, axis_index_groups=groups)  4.03 us
    unnamed x16, local copies, waits for them, and re-layouts  3.16 us
    pallas_call x1, Pallas kernels, do_public(): call(public_kernel, outs, [SM, VM, VM, ANY], scratch, 10 ** 9, 2 ** 21, [...  2.53 us
    pallas_call x1, Pallas kernels, do_grads(): call(grads_kernel, [(grads.shape, bf16), GRID16], [VM] * 3, (), 2 * 10 **...  2.28 us
    pallas_call x1, Pallas kernels, do_base(): call(base_kernel, outs, [SM] + [VM] * 6, [ROOM32], 10 ** 9, 2 ** 22)  1.8 us
    pallas_call x1, Pallas kernels, do_weights(): call(weights_kernel, outs, [SM] + [VM] * 4, [ROOM32], 3 * 10 ** 8, 2 ** 21)  1.63 us
  transfers between devices with their start and end apart: 5, of which 3 were waited for; matrix products, arithmetic and copies ran while one was open for 0% of the time, Pallas kernels for 17%

profile of v4, /device:TPU:1, one launch (start us, length us, event | category | flops | bytes accessed | tf_op | source)
XLA Modules:
  0.0 51.5 jit_solution(8286465240444562512)
XLA Ops:
  0.0 11.5 %collective-permute-start.21 = (bf16[128,256]{1,0:T(8,128)(2,1)}, bf16[128,256]{1,0:T(8,128)(2,1)S(1)}, u32[]{:S(2)}, u32[]{:S(2)}) collective-permute-start(bf16[128,256]{1,0:T(8,128)(2,1)} %bitcast.51), channel_id=1, source_target_pairs={{0,1},{1,0},{2,3},{3,2},{4,5},{5,4},{6,7},{7,6},{8,9},{9,8},{10,11... | collective-permute-start | bytes 196616 | tf_op jit(solution)/shard_map/ppermute | solution.py:354
  11.5 0.0 copy-start.3
  11.5 0.0 copy-start.5
  11.5 0.6 %copy-done.3 = s32[2]{0:T(128)S(1)} copy-done((s32[2]{0:T(128)S(1)}, s32[2]{0:T(128)}, u32[]{:S(2)}) %copy-start.3) | copy-done | bytes 32
  12.1 0.0 copy-done.5
  12.1 0.0 copy-start.1
  12.1 0.9 %copy-done.1 = bf16[1,256,512]{2,1,0:T(8,128)(2,1)S(1)} copy-done((bf16[1,256,512]{2,1,0:T(8,128)(2,1)S(1)}, bf16[1,256,512]{2,1,0:T(8,128)(2,1)}, u32[]{:S(2)}) %copy-start.1) | copy-done | bytes 262168
  13.1 0.8 %copy-done.2 = bf16[1,128,256]{2,1,0:T(8,128)(2,1)S(1)} copy-done((bf16[1,128,256]{2,1,0:T(8,128)(2,1)S(1)}, bf16[1,128,256]{2,1,0:T(8,128)(2,1)}, u32[]{:S(2)}) %copy-start.2) | copy-done | bytes 65560
  13.9 2.5 %shard_map.83 = (f32[64,16,128]{2,1,0:T(8,128)}, bf16[64,16,128]{2,1,0:T(8,128)(2,1)S(1)}, bf16[25,16,128]{2,1,0:T(8,128)(2,1)S(1)}, bf16[4,2,128,256]{3,2,1,0:T(8,128)(2,1)}, s32[1]{0:T(128)}) custom-call(s32[2]{0:T(128)S(1)} %copy-done.3, s32[1,40]{1,0:T(1,128)S(1)} %bitcast.63, bf16[256,512]{1,0:T(8,128)(2,1)S(1)} %bitcast.50, bf16[128,256]{1,0:T(8,128)(2,1)S(1)} %bitcast.52), custom_call_target="tpu_custom_call" | custom-call | flops 1000000000 | bytes 2097152 | tf_op jit(solution)/shard_map/pallas_call | solution.py:310
  16.5 0.0 collective-permute-done.21.other
  16.5 0.0 copy-start
  16.5 0.7 %shard_map.84 = bf16[4,2,128,256]{3,2,1,0:T(8,128)(2,1)} custom-call(bf16[128,256]{1,0:T(8,128)(2,1)S(1)} %collective-permute-done.21.other, bf16[4,2,128,256]{3,2,1,0:T(8,128)(2,1)} %get-tuple-element.312.pairs), custom_call_target="tpu_custom_call", output_to_operand_aliasing={{}: (1, {})} | custom-call | flops 100000 | bytes 1048576 | tf_op jit(solution)/shard_map/pallas_call | solution.py:315
  17.2 4.0 %all-to-all-start = ((bf16[4,2,128,256]{3,2,1,0:T(8,128)(2,1)}), bf16[4,2,128,256]{3,2,1,0:T(8,128)(2,1)S(1)}, u32[]{:S(2)}, u32[]{:S(2)}) async-start(bf16[4,2,128,256]{3,2,1,0:T(8,128)(2,1)} %shard_map.84), calls=%async_computation | async-start | bytes 1048576 | tf_op jit(solution)/shard_map/all_to_all | solution.py:372
  21.2 4.0 %collective-permute-start.20 = (bf16[25,16,128]{2,1,0:T(8,128)(2,1)S(1)}, bf16[25,16,128]{2,1,0:T(8,128)(2,1)S(1)}, u32[]{:S(2)}, u32[]{:S(2)}) collective-permute-start(bf16[25,16,128]{2,1,0:T(8,128)(2,1)S(1)} %get-tuple-element.311), channel_id=1, source_target_pairs={{0,256},{8,264},{16,272},{24,280},{32,288},{40,296},{48,304},{56,3... | collective-permute-start | bytes 307208 | tf_op jit(solution)/shard_map/ppermute | solution.py:354
  25.9 0.0 copy-done
  25.9 2.3 %shard_map.85 = (bf16[1024,512]{1,0:T(8,128)(2,1)S(1)}, bf16[256,512]{1,0:T(8,128)(2,1)S(1)}) custom-call(s32[1,1]{1,0:T(1,128)} %bitcast.48.count, bf16[1024,512]{1,0:T(8,128)(2,1)S(1)} %bitcast.49, bf16[256,512]{1,0:T(8,128)(2,1)} %bitcast.75), custom_call_target="tpu_custom_call" | custom-call | flops 2000000000 | bytes 4194304 | tf_op jit(solution)/shard_map/pallas_call | solution.py:319
  28.8 0.4 all-to-all-done.acts
  29.2 1.6 %shard_map.86 = (bf16[40,16,128]{2,1,0:T(8,128)(2,1)S(1)}, bf16[64,16,128]{2,1,0:T(8,128)(2,1)S(1)}, f32[40,16,128]{2,1,0:T(8,128)S(1)}, f32[256,512]{1,0:T(8,128)S(1)}) custom-call(s32[40]{0:T(128)S(1)} %bitcast.64, bf16[4,2,128,256]{3,2,1,0:T(8,128)(2,1)S(1)} %all-to-all-done.acts, bf16[1024,512]{1,0:T(8,128)(2,1)S(1)} %get-tuple-element.315.turned, ...), custom_call_target="tpu_custom_call" | custom-call | flops 300000000 | bytes 2097152 | tf_op jit(solution)/shard_map/pallas_call | solution.py:324
  30.9 0.0 collective-permute-done.20
  30.9 0.0 copy-done.6
  30.9 0.0 copy-done.7
  30.9 19.9 %conditional.1 = (bf16[1,256,512]{2,1,0:T(8,128)(2,1)S(1)}) conditional(s32[]{:T(128)} %bitcast.33, (bf16[25,16,128]{2,1,0:T(8,128)(2,1)S(1)}, bf16[64,16,128]{2,1,0:T(8,128)(2,1)S(1)}, s32[40]{0:T(128)S(1)}, f32[40,16,128]{2,1,0:T(8,128)S(1)}, f32[64,16,128]{2,1,0:T(8,128)S(1)}, /*index=5*/f32[256,512]{1,0:T(8,128)S(1)}, ...), branch_computations={%region_0.0_spmd, %region_1.0_spmd, %region_2.0_spmd, %region_3.0_... | conditional | flops 1202000128 | bytes 7733720 | solution.py:393
  30.9 4.4 %collective-permute-start = (bf16[64,16,128]{2,1,0:T(8,128)(2,1)S(1)}, bf16[64,16,128]{2,1,0:T(8,128)(2,1)S(1)}, u32[]{:S(2)}, u32[]{:S(2)}) collective-permute-start(bf16[64,16,128]{2,1,0:T(8,128)(2,1)S(1)} %get-tuple-element.158.own), channel_id=1, source_target_pairs={{0,8},{8,0},{16,24},{24,16},{32,40},{40,32},{48,56},{56,48},{64,72... | collective-permute-start | bytes 786440 | tf_op jit(solution)/shard_map/cond/branch_0_fun/ppermute | solution.py:354
  35.3 1.1 %collective-permute-done.peer = bf16[64,16,128]{2,1,0:T(8,128)(2,1)S(1)} collective-permute-done((bf16[64,16,128]{2,1,0:T(8,128)(2,1)S(1)}, bf16[64,16,128]{2,1,0:T(8,128)(2,1)S(1)}, u32[]{:S(2)}, u32[]{:S(2)}) %collective-permute-start) | collective-permute-done | bytes 262176 | tf_op jit(solution)/shard_map/cond/branch_0_fun/ppermute | solution.py:354
  36.4 1.3 %branch_0_fun.4 = (bf16[40,16,128]{2,1,0:T(8,128)(2,1)S(1)}, bf16[64,16,128]{2,1,0:T(8,128)(2,1)}, f32[40,16,128]{2,1,0:T(8,128)S(1)}) custom-call(s32[40]{0:T(128)S(1)} %get-tuple-element.157.kept, bf16[64,16,128]{2,1,0:T(8,128)(2,1)S(1)} %collective-permute-done.peer, bf16[64,16,128]{2,1,0:T(8,128)(2,1)S(1)} %get-tuple-element.158.own, ...), custom_call_target="tpu_custom_call" | custom-call | flops 1000000 | bytes 524288 | tf_op jit(solution)/shard_map/cond/branch_0_fun/pallas_call | solution.py:332
  37.8 4.0 %collective-permute-start.1 = (bf16[40,16,128]{2,1,0:T(8,128)(2,1)S(1)}, bf16[40,16,128]{2,1,0:T(8,128)(2,1)S(1)}, u32[]{:S(2)}, u32[]{:S(2)}) collective-permute-start(bf16[40,16,128]{2,1,0:T(8,128)(2,1)S(1)} %get-tuple-element.160), channel_id=1, source_target_pairs={{0,256},{8,264},{16,272},{24,280},{32,288},{40,296},{48,304},{56,3... | collective-permute-start | bytes 491528 | tf_op jit(solution)/shard_map/cond/branch_0_fun/ppermute | solution.py:354
  41.8 0.6 %branch_0_fun.5.filled = bf16[64,16,128]{2,1,0:T(8,128)(2,1)S(1)} custom-call(s32[64]{0:T(128)S(1)} %bitcast_convert_fusion.listed, bf16[25,16,128]{2,1,0:T(8,128)(2,1)S(1)} %get-tuple-element.156.early), custom_call_target="tpu_custom_call" | custom-call | flops 1000000 | bytes 262144 | tf_op jit(solution)/shard_map/cond/branch_0_fun/pallas_call | solution.py:328
  42.4 1.8 %branch_0_fun.6 = (f32[256,512]{1,0:T(8,128)S(1)}, bf16[128,128]{1,0:T(8,128)(2,1)S(1)}, bf16[512,512]{1,0:T(8,128)(2,1)S(1)}) custom-call(s32[40]{0:T(128)S(1)} %get-tuple-element.157.kept, bf16[64,16,128]{2,1,0:T(8,128)(2,1)S(1)} %collective-permute-done.peer, f32[64,16,128]{2,1,0:T(8,128)S(1)} %get-tuple-element.170.coeffs, ...), custom_call_target="tpu_custom_call" | custom-call | flops 1000000000 | bytes 4194304 | tf_op jit(solution)/shard_map/cond/branch_0_fun/pallas_call | solution.py:341
  44.2 5.3 %collective-permute-done.1.arrived = bf16[40,16,128]{2,1,0:T(8,128)(2,1)S(1)} collective-permute-done((bf16[40,16,128]{2,1,0:T(8,128)(2,1)S(1)}, bf16[40,16,128]{2,1,0:T(8,128)(2,1)S(1)}, u32[]{:S(2)}, u32[]{:S(2)}) %collective-permute-start.1) | collective-permute-done | bytes 163872 | tf_op jit(solution)/shard_map/cond/branch_0_fun/ppermute | solution.py:354
  49.5 1.1 %branch_0_fun.7 = bf16[256,512]{1,0:T(8,128)(2,1)S(1)} custom-call(s32[64]{0:T(128)S(1)} %bitcast_convert_fusion.listed, bf16[40,16,128]{2,1,0:T(8,128)(2,1)S(1)} %collective-permute-done.1.arrived, bf16[64,16,128]{2,1,0:T(8,128)(2,1)S(1)} %branch_0_fun.5.filled, f32[256,512]{1,0:T(8,128)S(1)} %get-tuple-element.176.base, ...), custom_call_target="tpu_custom_call" | custom-call | flops 200000000 | bytes 1048576 | tf_op jit(solution)/shard_map/cond/branch_0_fun/pallas_call | solution.py:349
  50.8 0.0 copy-start.4
  50.8 0.7 %copy-done.4 = bf16[1,256,512]{2,1,0:T(8,128)(2,1)} copy-done((bf16[1,256,512]{2,1,0:T(8,128)(2,1)}, bf16[1,256,512]{2,1,0:T(8,128)(2,1)S(1)}, u32[]{:S(2)}) %copy-start.4) | copy-done | bytes 262168
  (4 shorter events, 0.0 us)
Async XLA Ops:
  0.0 16.5 %collective-permute-start.21 = (bf16[128,256]{1,0:T(8,128)(2,1)}, bf16[128,256]{1,0:T(8,128)(2,1)S(1)}, u32[]{:S(2)}, u32[]{:S(2)}) collective-permute-start(bf16[128,256]{1,0:T(8,128)(2,1)} %bitcast.51), channel_id=1, source_target_pairs={{0,1},{1,0},{2,3},{3,2},{4,5},{5,4},{6,7},{7,6},{8,9},{9,8},{10,11... | collective-permute-start | bytes 196616 | tf_op jit(solution)/shard_map/ppermute | solution.py:354
  11.5 0.7 %copy-start.3 = (s32[2]{0:T(128)S(1)}, s32[2]{0:T(128)}, u32[]{:S(2)}) copy-start(s32[2]{0:T(128)} %distances.1) | copy-start | bytes 28
  11.5 0.7 %copy-start.5 = (s32[1,1,40]{2,1,0:T(1,128)S(1)}, s32[1,1,40]{2,1,0:T(1,128)}, u32[]{:S(2)}) copy-start(s32[1,1,40]{2,1,0:T(1,128)} %param.22) | copy-start | bytes 484
  12.1 0.9 %copy-start.1 = (bf16[1,256,512]{2,1,0:T(8,128)(2,1)S(1)}, bf16[1,256,512]{2,1,0:T(8,128)(2,1)}, u32[]{:S(2)}) copy-start(bf16[1,256,512]{2,1,0:T(8,128)(2,1)} %param.20) | copy-start | bytes 786436
  13.1 0.8 %copy-start.2 = (bf16[1,128,256]{2,1,0:T(8,128)(2,1)S(1)}, bf16[1,128,256]{2,1,0:T(8,128)(2,1)}, u32[]{:S(2)}) copy-start(bf16[1,128,256]{2,1,0:T(8,128)(2,1)} %param.17) | copy-start | bytes 196612
  16.5 9.4 %copy-start = (bf16[1,1024,512]{2,1,0:T(8,128)(2,1)S(1)}, bf16[1,1024,512]{2,1,0:T(8,128)(2,1)}, u32[]{:S(2)}) copy-start(bf16[1,1024,512]{2,1,0:T(8,128)(2,1)} %param.18) | copy-start | bytes 3145732
  17.2 12.0 %all-to-all-start = ((bf16[4,2,128,256]{3,2,1,0:T(8,128)(2,1)}), bf16[4,2,128,256]{3,2,1,0:T(8,128)(2,1)S(1)}, u32[]{:S(2)}, u32[]{:S(2)}) async-start(bf16[4,2,128,256]{3,2,1,0:T(8,128)(2,1)} %shard_map.84), calls=%async_computation | async-start | bytes 1048576 | tf_op jit(solution)/shard_map/all_to_all | solution.py:372
  21.2 9.6 %collective-permute-start.20 = (bf16[25,16,128]{2,1,0:T(8,128)(2,1)S(1)}, bf16[25,16,128]{2,1,0:T(8,128)(2,1)S(1)}, u32[]{:S(2)}, u32[]{:S(2)}) collective-permute-start(bf16[25,16,128]{2,1,0:T(8,128)(2,1)S(1)} %get-tuple-element.311), channel_id=1, source_target_pairs={{0,256},{8,264},{16,272},{24,280},{32,288},{40,296},{48,304},{56,3... | collective-permute-start | bytes 307208 | tf_op jit(solution)/shard_map/ppermute | solution.py:354
  29.2 1.7 %copy-start.6 = (bf16[1,256,512]{2,1,0:T(8,128)(2,1)S(1)}, bf16[1,256,512]{2,1,0:T(8,128)(2,1)}, u32[]{:S(2)}) copy-start(bf16[1,256,512]{2,1,0:T(8,128)(2,1)} %param.19) | copy-start | bytes 786436
  29.2 1.7 %copy-start.7 = (f32[64,16,128]{2,1,0:T(8,128)S(1)}, f32[64,16,128]{2,1,0:T(8,128)}, u32[]{:S(2)}) copy-start(f32[64,16,128]{2,1,0:T(8,128)} %get-tuple-element.320) | copy-start | bytes 1572868
  30.9 5.5 %collective-permute-start = (bf16[64,16,128]{2,1,0:T(8,128)(2,1)S(1)}, bf16[64,16,128]{2,1,0:T(8,128)(2,1)S(1)}, u32[]{:S(2)}, u32[]{:S(2)}) collective-permute-start(bf16[64,16,128]{2,1,0:T(8,128)(2,1)S(1)} %get-tuple-element.158.own), channel_id=1, source_target_pairs={{0,8},{8,0},{16,24},{24,16},{32,40},{40,32},{48,56},{56,48},{64,72... | collective-permute-start | bytes 786440 | tf_op jit(solution)/shard_map/cond/branch_0_fun/ppermute | solution.py:354
  37.8 11.7 %collective-permute-start.1 = (bf16[40,16,128]{2,1,0:T(8,128)(2,1)S(1)}, bf16[40,16,128]{2,1,0:T(8,128)(2,1)S(1)}, u32[]{:S(2)}, u32[]{:S(2)}) collective-permute-start(bf16[40,16,128]{2,1,0:T(8,128)(2,1)S(1)} %get-tuple-element.160), channel_id=1, source_target_pairs={{0,256},{8,264},{16,272},{24,280},{32,288},{40,296},{48,304},{56,3... | collective-permute-start | bytes 491528 | tf_op jit(solution)/shard_map/cond/branch_0_fun/ppermute | solution.py:354
  50.8 0.7 %copy-start.4 = (bf16[1,256,512]{2,1,0:T(8,128)(2,1)}, bf16[1,256,512]{2,1,0:T(8,128)(2,1)S(1)}, u32[]{:S(2)}) copy-start(bf16[1,256,512]{2,1,0:T(8,128)(2,1)S(1)} %get-tuple-element.374) | copy-start | bytes 786436

commit v5 on v4

--- a/solution.py
+++ b/solution.py
@@ -11,6 +11,7 @@
 step = 0.25
 ROWS, COLS, KEEP, SLABS, TOP = 256, 512, 40, 64, 5
 LEFT = SLABS - KEEP
+PACKED = (2, 3, TOP)
 f32, bf16, i32 = jnp.float32, jnp.bfloat16, jnp.int32
 VM = pl.BlockSpec(memory_space=pltpu.VMEM)
 SM = pl.BlockSpec(memory_space=pltpu.SMEM)
@@ -359,14 +360,13 @@
 
 
 def shards(activations, out_grads, weight, public, counts, kept, distances):
-    top = TOP
     count_x = lax.axis_size("tp") // 2
     groups = [[2 * x + z for x in range(count_x)] for z in range(2)]
     acts, grads, weight, public, kept = activations[0], out_grads[0], weight[0], public[0], kept[0, 0]
 
     other = swapped(acts, "tp", 0)
     coeffs, public_full, early, pairs, way = do_public(count_x, distances, kept[None], public, acts)
-    early_far = swapped(early, "rep", top)
+    early_far = swapped(early, "rep", TOP)
     pairs = do_spread(other, pairs)
     pairs, counts = lax.optimization_barrier((pairs, counts[:, None]))
     rows = lax.all_to_all(pairs, "tp", 0, 0, axis_index_groups=groups)
@@ -374,23 +374,29 @@
     packed, full, kept_coeffs, moved = do_weights(kept, rows, turned, weight_turned, public_full)
 
     def rounds(first, second):
-        def run(packed, full, early_far):
-            listed = peers_list(early_far)
-            filled = do_fill(listed, early_far)
-            if first == top:
-                packed, full, next_coeffs, peer = do_far(kept, listed, swapped(packed, "rep", first), filled, full, kept_coeffs)
+        def run(packed, full, early, early_far):
+            if first == TOP:
+                arrived = swapped(packed, "rep", first)
+                if second in PACKED:
+                    early, packed = lax.optimization_barrier((early, packed))
+                    early_second = swapped(early, "rep", second)
+                listed = peers_list(early_far)
+                filled = do_fill(listed, early_far)
+                packed, full, next_coeffs, peer = do_far(kept, listed, arrived, filled, full, kept_coeffs)
             else:
+                early_second = early_far
                 packed, full, next_coeffs, peer = do_near(kept, swapped(full, "rep", first), full, kept_coeffs)
-            arrived = swapped(packed if second == top else full, "rep", second)
+            arrived = swapped(packed if second in PACKED else full, "rep", second)
             last = do_base(kept, peer, coeffs, kept_coeffs, next_coeffs, moved, weight)
-            if second == top:
-                return do_far_last(listed, arrived, filled, *last)
+            if second in PACKED:
+                listed = peers_list(early_second)
+                return do_far_last(listed, arrived, do_fill(listed, early_second), *last)
             return do_near_last(arrived, *last)
 
         return run
 
-    ways = [(bit, top) for bit in range(top)] + [(top, bit) for bit in range(top)]
-    return lax.switch(way[0], [rounds(*pair) for pair in ways], packed, full, early_far)[None]
+    ways = [(bit, TOP) for bit in range(TOP)] + [(TOP, bit) for bit in range(TOP)]
+    return lax.switch(way[0], [rounds(*pair) for pair in ways], packed, full, early, early_far)[None]
 
 
 def solution(mesh):

time: 51.9 us -> 51.1 us (0.985)
  Pallas kernels: 12 us -> 10.5 us
  waiting for transfers between devices: 6.81 us -> 8 us
  starting transfers between devices: 27.8 us -> 27.1 us
    pallas_call x1, Pallas kernels: 2.28 us -> 1.33 us  [do_grads(): call(grads_kernel, [(grads.shape, bf16), GRID16], [VM] * 3, (), 2 * 10 **...]
    all_to_all x1, waiting for transfers between devices: 0.39 us -> 1.32 us  [shards(): rows = lax.all_to_all(pairs, 'tp', 0, 0, axis_index_groups=groups)]
    ppermute x4, starting transfers between devices: 23.8 us -> 23 us  [swapped(): return lax.ppermute(block, axis, [(i, i ^ 1 << bit) for i in range(count)])]
    pallas_call x2, Pallas kernels: 2.41 us -> 1.84 us  [the longest x1 1.32 us: do_far(): call(far_kernel, [KEPT16, SLAB16, KEPT32, SLAB16], [SM, SM] + [VM] * 4, (...]
  transfers between devices with their start and end apart: 5 -> 5, of which waited for: 3 -> 2; matrix products, arithmetic and copies ran while one was open for 0% -> 0% of each run, Pallas kernels for 17% -> 16%
where the time goes in v5:
time: 51.1 us; the launch traced here: 50.8 us
  starting transfers between devices  27.1 us (53%)
  Pallas kernels  10.5 us (21%)
  waiting for transfers between devices  8 us (16%)
  local copies, waits for them, and re-layouts  3.16 us (6%)
  between operations  1.44 us (3%)
    ppermute x4, starting transfers between devices, swapped(): return lax.ppermute(block, axis, [(i, i ^ 1 << bit) for i in range(count)])  23 us
    ppermute x4, waiting for transfers between devices, swapped(): return lax.ppermute(block, axis, [(i, i ^ 1 << bit) for i in range(count)])  6.68 us
    all_to_all x1, starting transfers between devices, shards(): rows = lax.all_to_all(pairs, 'tp', 0, 0, axis_index_groups=groups)  4.16 us
    unnamed x16, local copies, waits for them, and re-layouts  3.16 us
    pallas_call x1, Pallas kernels, do_public(): call(public_kernel, outs, [SM, VM, VM, ANY], scratch, 10 ** 9, 2 ** 21, [...  2.59 us
    pallas_call x1, Pallas kernels, do_base(): call(base_kernel, outs, [SM] + [VM] * 6, [ROOM32], 10 ** 9, 2 ** 22)  1.81 us
    pallas_call x1, Pallas kernels, do_weights(): call(weights_kernel, outs, [SM] + [VM] * 4, [ROOM32], 3 * 10 ** 8, 2 ** 21)  1.63 us
    pallas_call x1, Pallas kernels, do_grads(): call(grads_kernel, [(grads.shape, bf16), GRID16], [VM] * 3, (), 2 * 10 **...  1.33 us
  transfers between devices with their start and end apart: 5, of which 2 were waited for; matrix products, arithmetic and copies ran while one was open for 0% of the time, Pallas kernels for 16%

profile of v5, /device:TPU:1, one launch (start us, length us, event | category | flops | bytes accessed | tf_op | source)
XLA Modules:
  0.0 50.8 jit_solution(16507598253699584220)
XLA Ops:
  0.0 11.5 %collective-permute-start.23 = (bf16[128,256]{1,0:T(8,128)(2,1)}, bf16[128,256]{1,0:T(8,128)(2,1)S(1)}, u32[]{:S(2)}, u32[]{:S(2)}) collective-permute-start(bf16[128,256]{1,0:T(8,128)(2,1)} %bitcast.61), channel_id=1, source_target_pairs={{0,1},{1,0},{2,3},{3,2},{4,5},{5,4},{6,7},{7,6},{8,9},{9,8},{10,11... | collective-permute-start | bytes 196616 | tf_op jit(solution)/shard_map/ppermute | solution.py:355
  11.5 0.0 copy-start.3
  11.5 0.0 copy-start.5
  11.5 0.6 %copy-done.3 = s32[2]{0:T(128)S(1)} copy-done((s32[2]{0:T(128)S(1)}, s32[2]{0:T(128)}, u32[]{:S(2)}) %copy-start.3) | copy-done | bytes 32
  12.1 0.0 copy-done.5
  12.1 0.9 %copy-done.1 = bf16[1,256,512]{2,1,0:T(8,128)(2,1)S(1)} copy-done((bf16[1,256,512]{2,1,0:T(8,128)(2,1)S(1)}, bf16[1,256,512]{2,1,0:T(8,128)(2,1)}, u32[]{:S(2)}) %copy-start.1) | copy-done | bytes 262168
  13.1 0.8 %copy-done.2 = bf16[1,128,256]{2,1,0:T(8,128)(2,1)S(1)} copy-done((bf16[1,128,256]{2,1,0:T(8,128)(2,1)S(1)}, bf16[1,128,256]{2,1,0:T(8,128)(2,1)}, u32[]{:S(2)}) %copy-start.2) | copy-done | bytes 65560
  13.9 2.6 %shard_map.83 = (f32[64,16,128]{2,1,0:T(8,128)}, bf16[64,16,128]{2,1,0:T(8,128)(2,1)S(1)}, bf16[25,16,128]{2,1,0:T(8,128)(2,1)}, bf16[4,2,128,256]{3,2,1,0:T(8,128)(2,1)}, s32[1]{0:T(128)}) custom-call(s32[2]{0:T(128)S(1)} %copy-done.3, s32[1,40]{1,0:T(1,128)S(1)} %bitcast.73, bf16[256,512]{1,0:T(8,128)(2,1)S(1)} %bitcast.60, bf16[128,256]{1,0:T(8,128)(2,1)S(1)} %bitcast.62), custom_call_target="tpu_custom_call" | custom-call | flops 1000000000 | bytes 2097152 | tf_op jit(solution)/shard_map/pallas_call | solution.py:311
  16.5 0.0 collective-permute-done.23.other
  16.5 0.0 copy-start
  16.5 0.7 %shard_map.84 = bf16[4,2,128,256]{3,2,1,0:T(8,128)(2,1)} custom-call(bf16[128,256]{1,0:T(8,128)(2,1)S(1)} %collective-permute-done.23.other, bf16[4,2,128,256]{3,2,1,0:T(8,128)(2,1)} %get-tuple-element.320.pairs), custom_call_target="tpu_custom_call", output_to_operand_aliasing={{}: (1, {})} | custom-call | flops 100000 | bytes 1048576 | tf_op jit(solution)/shard_map/pallas_call | solution.py:316
  17.3 0.0 copy-start.6
  17.3 4.2 %all-to-all-start = ((bf16[4,2,128,256]{3,2,1,0:T(8,128)(2,1)}), bf16[4,2,128,256]{3,2,1,0:T(8,128)(2,1)S(1)}, u32[]{:S(2)}, u32[]{:S(2)}) async-start(bf16[4,2,128,256]{3,2,1,0:T(8,128)(2,1)} %shard_map.84), calls=%async_computation | async-start | bytes 1048576 | tf_op jit(solution)/shard_map/all_to_all | solution.py:372
  21.5 4.0 %collective-permute-start.22 = (bf16[25,16,128]{2,1,0:T(8,128)(2,1)}, bf16[25,16,128]{2,1,0:T(8,128)(2,1)S(1)}, u32[]{:S(2)}, u32[]{:S(2)}) collective-permute-start(bf16[25,16,128]{2,1,0:T(8,128)(2,1)} %get-tuple-element.319), channel_id=1, source_target_pairs={{0,256},{8,264},{16,272},{24,280},{32,288},{40,296},{48,304},{56,3... | collective-permute-start | bytes 307208 | tf_op jit(solution)/shard_map/ppermute | solution.py:355
  26.1 0.0 copy-done
  26.1 0.0 copy-done.6
  26.1 1.3 %shard_map.85 = (bf16[1024,512]{1,0:T(8,128)(2,1)S(1)}, bf16[256,512]{1,0:T(8,128)(2,1)S(1)}) custom-call(s32[1,1]{1,0:T(1,128)} %bitcast.58.count, bf16[1024,512]{1,0:T(8,128)(2,1)S(1)} %bitcast.59, bf16[256,512]{1,0:T(8,128)(2,1)S(1)} %bitcast.85), custom_call_target="tpu_custom_call" | custom-call | flops 2000000000 | bytes 4194304 | tf_op jit(solution)/shard_map/pallas_call | solution.py:320
  28.1 1.3 %all-to-all-done.acts = bf16[4,2,128,256]{3,2,1,0:T(8,128)(2,1)S(1)} async-done(((bf16[4,2,128,256]{3,2,1,0:T(8,128)(2,1)}), bf16[4,2,128,256]{3,2,1,0:T(8,128)(2,1)S(1)}, u32[]{:S(2)}, u32[]{:S(2)}) %all-to-all-start) | async-done | bytes 524320 | tf_op jit(solution)/shard_map/all_to_all | solution.py:372
  29.4 1.6 %shard_map.86 = (bf16[40,16,128]{2,1,0:T(8,128)(2,1)S(1)}, bf16[64,16,128]{2,1,0:T(8,128)(2,1)S(1)}, f32[40,16,128]{2,1,0:T(8,128)S(1)}, f32[256,512]{1,0:T(8,128)S(1)}) custom-call(s32[40]{0:T(128)S(1)} %bitcast.74, bf16[4,2,128,256]{3,2,1,0:T(8,128)(2,1)S(1)} %all-to-all-done.acts, bf16[1024,512]{1,0:T(8,128)(2,1)S(1)} %get-tuple-element.323.turned, ...), custom_call_target="tpu_custom_call" | custom-call | flops 300000000 | bytes 2097152 | tf_op jit(solution)/shard_map/pallas_call | solution.py:325
  31.1 0.0 collective-permute-done.22
  31.1 0.0 copy-done.7
  31.1 18.9 %conditional.1 = (bf16[1,256,512]{2,1,0:T(8,128)(2,1)S(1)}) conditional(s32[]{:T(128)} %bitcast.37, (bf16[25,16,128]{2,1,0:T(8,128)(2,1)S(1)}, bf16[64,16,128]{2,1,0:T(8,128)(2,1)S(1)}, s32[40]{0:T(128)S(1)}, f32[40,16,128]{2,1,0:T(8,128)S(1)}, f32[64,16,128]{2,1,0:T(8,128)S(1)}, /*index=5*/f32[256,512]{1,0:T(8,128)S(1)}, ...), branch_computations={%region_0.0_spmd, %region_1.0_spmd, %region_2.0_spmd, %region_3.0_... | conditional | flops 1203000064 | bytes 8012672 | solution.py:399
  31.1 4.0 %collective-permute-start.10 = (bf16[40,16,128]{2,1,0:T(8,128)(2,1)S(1)}, bf16[40,16,128]{2,1,0:T(8,128)(2,1)S(1)}, u32[]{:S(2)}, u32[]{:S(2)}) collective-permute-start(bf16[40,16,128]{2,1,0:T(8,128)(2,1)S(1)} %get-tuple-element.233), channel_id=1, source_target_pairs={{0,256},{8,264},{16,272},{24,280},{32,288},{40,296},{48,304},{56,3... | collective-permute-start | bytes 491528 | tf_op jit(solution)/shard_map/cond/branch_5_fun/ppermute | solution.py:355
  35.2 0.6 %branch_5_fun.4.filled = bf16[64,16,128]{2,1,0:T(8,128)(2,1)S(1)} custom-call(s32[64]{0:T(128)S(1)} %bitcast_convert_fusion.5.listed, bf16[25,16,128]{2,1,0:T(8,128)(2,1)S(1)} %get-tuple-element.232.early), custom_call_target="tpu_custom_call" | custom-call | flops 1000000 | bytes 262144 | tf_op jit(solution)/shard_map/cond/branch_5_fun/pallas_call | solution.py:329
  35.8 6.7 %collective-permute-done.10.arrived = bf16[40,16,128]{2,1,0:T(8,128)(2,1)S(1)} collective-permute-done((bf16[40,16,128]{2,1,0:T(8,128)(2,1)S(1)}, bf16[40,16,128]{2,1,0:T(8,128)(2,1)S(1)}, u32[]{:S(2)}, u32[]{:S(2)}) %collective-permute-start.10) | collective-permute-done | bytes 163872 | tf_op jit(solution)/shard_map/cond/branch_5_fun/ppermute | solution.py:355
  42.4 1.3 %branch_5_fun.5 = (bf16[40,16,128]{2,1,0:T(8,128)(2,1)}, bf16[64,16,128]{2,1,0:T(8,128)(2,1)S(1)}, f32[40,16,128]{2,1,0:T(8,128)S(1)}, bf16[64,16,128]{2,1,0:T(8,128)(2,1)S(1)}) custom-call(s32[40]{0:T(128)S(1)} %get-tuple-element.231.kept, s32[64]{0:T(128)S(1)} %bitcast_convert_fusion.5.listed, bf16[40,16,128]{2,1,0:T(8,128)(2,1)S(1)} %collective-permute-done.10.arrived, ...), custom_call_target="tpu_custom_call" | custom-call | flops 1000000 | bytes 524288 | tf_op jit(solution)/shard_map/cond/branch_5_fun/pallas_call | solution.py:337
  43.8 3.5 %collective-permute-start.11 = (bf16[64,16,128]{2,1,0:T(8,128)(2,1)S(1)}, bf16[64,16,128]{2,1,0:T(8,128)(2,1)S(1)}, u32[]{:S(2)}, u32[]{:S(2)}) collective-permute-start(bf16[64,16,128]{2,1,0:T(8,128)(2,1)S(1)} %get-tuple-element.236), channel_id=1, source_target_pairs={{0,8},{8,0},{16,24},{24,16},{32,40},{40,32},{48,56},{56,48},{64,72... | collective-permute-start | bytes 786440 | tf_op jit(solution)/shard_map/cond/branch_5_fun/ppermute | solution.py:355
  47.3 1.8 %branch_5_fun.6 = (f32[256,512]{1,0:T(8,128)S(1)}, bf16[128,128]{1,0:T(8,128)(2,1)S(1)}, bf16[512,512]{1,0:T(8,128)(2,1)S(1)}) custom-call(s32[40]{0:T(128)S(1)} %get-tuple-element.231.kept, bf16[64,16,128]{2,1,0:T(8,128)(2,1)S(1)} %get-tuple-element.237.peer, f32[64,16,128]{2,1,0:T(8,128)S(1)} %get-tuple-element.238.coeffs, ...), custom_call_target="tpu_custom_call" | custom-call | flops 1000000000 | bytes 4194304 | tf_op jit(solution)/shard_map/cond/branch_5_fun/pallas_call | solution.py:342
  49.1 0.0 collective-permute-done.11.peer
  49.1 0.5 %branch_5_fun.7 = bf16[256,512]{1,0:T(8,128)(2,1)S(1)} custom-call(bf16[64,16,128]{2,1,0:T(8,128)(2,1)S(1)} %collective-permute-done.11.peer, f32[256,512]{1,0:T(8,128)S(1)} %get-tuple-element.242.base, bf16[128,128]{1,0:T(8,128)(2,1)S(1)} %get-tuple-element.243.left_t, bf16[512,512]{1,0:T(8,128)(2,1)S(1)} %get-tuple-element.244.right_t), custom_call_target="tpu_custom_call" | custom-call | flops 200000000 | bytes 1048576 | tf_op jit(solution)/shard_map/cond/branch_5_fun/pallas_call | solution.py:346
  50.1 0.0 copy-start.4
  50.1 0.7 %copy-done.4 = bf16[1,256,512]{2,1,0:T(8,128)(2,1)} copy-done((bf16[1,256,512]{2,1,0:T(8,128)(2,1)}, bf16[1,256,512]{2,1,0:T(8,128)(2,1)S(1)}, u32[]{:S(2)}) %copy-start.4) | copy-done | bytes 262168
  (4 shorter events, 0.0 us)
Async XLA Ops:
  0.0 16.5 %collective-permute-start.23 = (bf16[128,256]{1,0:T(8,128)(2,1)}, bf16[128,256]{1,0:T(8,128)(2,1)S(1)}, u32[]{:S(2)}, u32[]{:S(2)}) collective-permute-start(bf16[128,256]{1,0:T(8,128)(2,1)} %bitcast.61), channel_id=1, source_target_pairs={{0,1},{1,0},{2,3},{3,2},{4,5},{5,4},{6,7},{7,6},{8,9},{9,8},{10,11... | collective-permute-start | bytes 196616 | tf_op jit(solution)/shard_map/ppermute | solution.py:355
  11.5 0.7 %copy-start.3 = (s32[2]{0:T(128)S(1)}, s32[2]{0:T(128)}, u32[]{:S(2)}) copy-start(s32[2]{0:T(128)} %distances.1) | copy-start | bytes 28
  11.5 0.7 %copy-start.5 = (s32[1,1,40]{2,1,0:T(1,128)S(1)}, s32[1,1,40]{2,1,0:T(1,128)}, u32[]{:S(2)}) copy-start(s32[1,1,40]{2,1,0:T(1,128)} %param.22) | copy-start | bytes 484
  12.1 0.9 %copy-start.1 = (bf16[1,256,512]{2,1,0:T(8,128)(2,1)S(1)}, bf16[1,256,512]{2,1,0:T(8,128)(2,1)}, u32[]{:S(2)}) copy-start(bf16[1,256,512]{2,1,0:T(8,128)(2,1)} %param.20) | copy-start | bytes 786436
  13.1 0.8 %copy-start.2 = (bf16[1,128,256]{2,1,0:T(8,128)(2,1)S(1)}, bf16[1,128,256]{2,1,0:T(8,128)(2,1)}, u32[]{:S(2)}) copy-start(bf16[1,128,256]{2,1,0:T(8,128)(2,1)} %param.17) | copy-start | bytes 196612
  16.5 9.6 %copy-start = (bf16[1,1024,512]{2,1,0:T(8,128)(2,1)S(1)}, bf16[1,1024,512]{2,1,0:T(8,128)(2,1)}, u32[]{:S(2)}) copy-start(bf16[1,1024,512]{2,1,0:T(8,128)(2,1)} %param.18) | copy-start | bytes 3145732
  17.3 8.8 %copy-start.6 = (bf16[1,256,512]{2,1,0:T(8,128)(2,1)S(1)}, bf16[1,256,512]{2,1,0:T(8,128)(2,1)}, u32[]{:S(2)}) copy-start(bf16[1,256,512]{2,1,0:T(8,128)(2,1)} %param.19) | copy-start | bytes 786436
  17.3 12.1 %all-to-all-start = ((bf16[4,2,128,256]{3,2,1,0:T(8,128)(2,1)}), bf16[4,2,128,256]{3,2,1,0:T(8,128)(2,1)S(1)}, u32[]{:S(2)}, u32[]{:S(2)}) async-start(bf16[4,2,128,256]{3,2,1,0:T(8,128)(2,1)} %shard_map.84), calls=%async_computation | async-start | bytes 1048576 | tf_op jit(solution)/shard_map/all_to_all | solution.py:372
  21.5 9.6 %collective-permute-start.22 = (bf16[25,16,128]{2,1,0:T(8,128)(2,1)}, bf16[25,16,128]{2,1,0:T(8,128)(2,1)S(1)}, u32[]{:S(2)}, u32[]{:S(2)}) collective-permute-start(bf16[25,16,128]{2,1,0:T(8,128)(2,1)} %get-tuple-element.319), channel_id=1, source_target_pairs={{0,256},{8,264},{16,272},{24,280},{32,288},{40,296},{48,304},{56,3... | collective-permute-start | bytes 307208 | tf_op jit(solution)/shard_map/ppermute | solution.py:355
  29.4 1.7 %copy-start.7 = (f32[64,16,128]{2,1,0:T(8,128)S(1)}, f32[64,16,128]{2,1,0:T(8,128)}, u32[]{:S(2)}) copy-start(f32[64,16,128]{2,1,0:T(8,128)} %get-tuple-element.328) | copy-start | bytes 1572868
  31.1 11.3 %collective-permute-start.10 = (bf16[40,16,128]{2,1,0:T(8,128)(2,1)S(1)}, bf16[40,16,128]{2,1,0:T(8,128)(2,1)S(1)}, u32[]{:S(2)}, u32[]{:S(2)}) collective-permute-start(bf16[40,16,128]{2,1,0:T(8,128)(2,1)S(1)} %get-tuple-element.233), channel_id=1, source_target_pairs={{0,256},{8,264},{16,272},{24,280},{32,288},{40,296},{48,304},{56,3... | collective-permute-start | bytes 491528 | tf_op jit(solution)/shard_map/cond/branch_5_fun/ppermute | solution.py:355
  43.8 5.3 %collective-permute-start.11 = (bf16[64,16,128]{2,1,0:T(8,128)(2,1)S(1)}, bf16[64,16,128]{2,1,0:T(8,128)(2,1)S(1)}, u32[]{:S(2)}, u32[]{:S(2)}) collective-permute-start(bf16[64,16,128]{2,1,0:T(8,128)(2,1)S(1)} %get-tuple-element.236), channel_id=1, source_target_pairs={{0,8},{8,0},{16,24},{24,16},{32,40},{40,32},{48,56},{56,48},{64,72... | collective-permute-start | bytes 786440 | tf_op jit(solution)/shard_map/cond/branch_5_fun/ppermute | solution.py:355
  50.1 0.7 %copy-start.4 = (bf16[1,256,512]{2,1,0:T(8,128)(2,1)}, bf16[1,256,512]{2,1,0:T(8,128)(2,1)S(1)}, u32[]{:S(2)}) copy-start(bf16[1,256,512]{2,1,0:T(8,128)(2,1)S(1)} %get-tuple-element.383) | copy-start | bytes 786436
